TPU v7x, 256 devices: a whole 4x4x8 slice. The times are simulated.
256 devices in a mesh: rows: 64 (over x, z, core), cols: 4 (over y).
Axes of the slice: x: 4, y: 4, z: 8, core: 2. Of those that a mesh axis runs over, the one named last changes fastest.
Arguments:
- points: bfloat16 [128, 262144], P('cols', 'rows'), may hold values from -6 to 6
- basis: bfloat16 [4096, 64, 64], P('rows'), may hold values from -0.75 to 0.75
- leaf_transfer: bfloat16 [4096, 64, 64], P('rows'), may hold values from -0.5 to 0.5
- box_transfer: bfloat16 [512, 64, 64], P('rows'), may hold values from -0.5 to 0.5
- coarse_transfer: bfloat16 [96, 64, 64], replicated, may hold values from -0.5 to 0.5
- send_leaf: int32 [4096, 16], P('rows', 'cols'), may hold values from -1 to 63, as said below
- leaf_far: int32 [4096, 24], P('rows', 'cols'), may hold values from 0 to 255, as said below
- leaf_coupling: bfloat16 [4096, 24, 64, 64], P('rows', 'cols'), may hold values from -0.15625 to 0.15625
- send_box: int32 [4096, 8], P('rows', 'cols'), may hold values from -1 to 7, as said below
- box_far: int32 [512, 16], P('rows', 'cols'), may hold values from 0 to 127, as said below
- box_coupling: bfloat16 [512, 16, 64, 64], P('rows', 'cols'), may hold values from -0.09375 to 0.09375
- coarse_far: int32 [112, 8], P(None, 'cols'), may hold values from 0 to 111, as said below
- coarse_coupling: bfloat16 [112, 8, 64, 64], P(None, 'cols'), may hold values from -0.0625 to 0.0625
- near_index: int32 [4096, 8], P('rows'), may hold values from 0 to 4095, as said below
- near_block: bfloat16 [4096, 8, 64, 64], P('rows'), may hold values from -0.25 to 0.25
Outputs:
- product: bfloat16 [128, 262144], P('cols', 'rows')
Inputs may be any that keep to these rules, and one draw needn't show every extreme that they name: `send_leaf`: row p * 64 + d, columns q * 4 to q * 4 + 3: distinct leaf numbers within device p, live ones first and -1 after them; every such group has at least one live entry, and in every draw one device d receives a full 4 from every device p in some share. `leaf_far`: an entry in columns q * 6 onward of a leaf on device d is p * 4 + s with s a live position of row p * 64 + d, share q, of send_leaf. `send_box`: row p * 64 + d, columns q * 2 to q * 2 + 1: distinct box numbers within device p, live ones first and -1 after them; every such group has at least one live entry, and in every draw one device d receives a full 2 from every device p in some share. `box_far`: an entry in columns q * 4 onward of a box on device d is p * 2 + s with s a live position of row p * 64 + d, share q, of send_box. `coarse_far`: entries of node i name nodes of the same level as i (levels: indices below 16, below 48, the rest), never i itself; entries may repeat. `near_index`: entry 0 of leaf l is l itself; every entry names a leaf on the device of l or on a device next to it along rows.
All inputs are finite; a program needn't handle non-finite values.
Results may differ from a plain program's by a relative error of at most 0.0052.
Values may be sent and summed in bfloat16 or wider, within the bound.
A program may use at most 128 MiB of HBM per device.

v0:
```python
import jax
import jax.numpy as jnp
from jax import lax
from jax.sharding import PartitionSpec as P

HIGHEST = lax.Precision.HIGHEST


def padded(block, sides, width):
    for axis, dim in sides:
        count = lax.axis_size(axis)
        forward = [(i, i + 1) for i in range(count - 1)]
        backward = [(target, source) for source, target in forward]
        low = lax.ppermute(
            lax.slice_in_dim(block, block.shape[dim] - width, None, axis=dim), axis, forward
        )
        high = lax.ppermute(lax.slice_in_dim(block, 0, width, axis=dim), axis, backward)
        block = jnp.concatenate([low, block, high], axis=dim)
    return block


def widen(array):
    return array.astype(jnp.float32)


def lower_field(transfer, parent_field):
    return jnp.einsum("krs,kvs->kvr", widen(transfer), parent_field, precision=HIGHEST)


def outgoing(coef_full, table):
    flat = coef_full.reshape(coef_full.shape[0], -1)
    return jnp.take(flat, jnp.maximum(table, 0).reshape(-1), axis=0)


def body(
    points,
    basis,
    leaf_transfer,
    box_transfer,
    coarse_transfer,
    send_leaf,
    leaf_far,
    leaf_coupling,
    send_box,
    box_far,
    box_coupling,
    coarse_far,
    coarse_coupling,
    near_index,
    near_block,
):
    row_count = lax.axis_size("rows")
    own_index = lax.axis_index("rows")
    quarter = points.shape[0]
    vectors = quarter * lax.axis_size("cols")
    leaf_count, leaf_size, basis_rank = basis.shape
    box_count = box_transfer.shape[0]
    half_rows = row_count // 2
    quarter_rows = row_count // 4
    point_blocks = points.reshape(quarter, leaf_count, leaf_size)
    leaf_part = jnp.einsum(
        "vlb,lbr->lvr", point_blocks, basis, preferred_element_type=jnp.float32
    ).astype(jnp.bfloat16)
    leaf_full = lax.all_gather(leaf_part, "cols", axis=1, tiled=True)
    leaf_recv = lax.all_to_all(
        outgoing(leaf_full, send_leaf), "rows", split_axis=0, concat_axis=0, tiled=True
    )
    grouped = leaf_part.reshape(box_count, 8, leaf_part.shape[1], basis_rank)
    children = leaf_transfer.reshape(box_count, 8, basis_rank, basis_rank)
    boxes = jnp.einsum(
        "kjvr,kjrs->kvs", grouped, children, preferred_element_type=jnp.float32
    ).astype(jnp.bfloat16)
    device_root = jnp.einsum(
        "kvr,krs->vs", boxes, box_transfer, preferred_element_type=jnp.float32
    ).astype(jnp.bfloat16)
    box_full, root_full = (
        lax.all_gather(boxes, "cols", axis=1, tiled=True),
        lax.all_gather(device_root, "cols", axis=0, tiled=True),
    )
    box_recv = lax.all_to_all(
        outgoing(box_full, send_box), "rows", split_axis=0, concat_axis=0, tiled=True
    )

    def far_terms(received, slot_map, coupling):
        partner = jnp.take(received, slot_map.reshape(-1), axis=0)
        partner = partner.reshape(slot_map.shape[0], slot_map.shape[1], vectors, basis_rank)
        return jnp.einsum("lfrs,lfvs->lvr", coupling, partner, preferred_element_type=jnp.float32)

    far_leaf = far_terms(leaf_recv, leaf_far, leaf_coupling)
    far_box = far_terms(box_recv, box_far, box_coupling)
    roots_all = lax.all_gather(root_full[None], "rows", axis=0, tiled=True)
    coef_mid = jnp.einsum(
        "jtvr,jtrs->jvs",
        roots_all.reshape(half_rows, 2, vectors, basis_rank),
        coarse_transfer[half_rows:].reshape(half_rows, 2, basis_rank, basis_rank),
        preferred_element_type=jnp.float32,
    ).astype(jnp.bfloat16)
    coef_top = jnp.einsum(
        "jtvr,jtrs->jvs",
        coef_mid.reshape(quarter_rows, 2, vectors, basis_rank),
        coarse_transfer[:half_rows].reshape(quarter_rows, 2, basis_rank, basis_rank),
        preferred_element_type=jnp.float32,
    ).astype(jnp.bfloat16)
    coef_coarse = jnp.concatenate([coef_top, coef_mid, roots_all], axis=0)
    partner = jnp.take(coef_coarse, coarse_far.reshape(-1), axis=0)
    partner = partner.reshape(coarse_far.shape[0], coarse_far.shape[1], vectors, basis_rank)
    far_coarse = jnp.einsum(
        "ifrs,ifvs->ivr", coarse_coupling, partner, preferred_element_type=jnp.float32
    )
    field_top = far_coarse[:quarter_rows]
    field_mid = (
        lower_field(coarse_transfer[:half_rows], jnp.repeat(field_top, 2, axis=0))
        + far_coarse[quarter_rows : 3 * quarter_rows]
    )
    field_every = (
        lower_field(coarse_transfer[half_rows:], jnp.repeat(field_mid, 2, axis=0))
        + far_coarse[3 * quarter_rows :]
    )
    root_field = lax.dynamic_index_in_dim(field_every, own_index, 0, keepdims=False)
    field_box = (
        jnp.einsum("krs,vs->kvr", widen(box_transfer), root_field, precision=HIGHEST) + far_box
    )
    field_leaf = lower_field(leaf_transfer, jnp.repeat(field_box, 8, axis=0)) + far_leaf
    spread = jnp.einsum("lar,lvr->vla", widen(basis), field_leaf, precision=HIGHEST)
    far_mine = lax.psum_scatter(
        spread.reshape(field_leaf.shape[1], -1), "cols", scatter_dimension=0, tiled=True
    )
    extended = padded(points, (("rows", 1),), leaf_count * leaf_size)
    local_ids = near_index - (own_index - 1) * leaf_count
    extended_blocks = extended.reshape(quarter, 3 * leaf_count, leaf_size)
    picked = jnp.take(extended_blocks, local_ids.reshape(-1), axis=1)
    picked = picked.reshape(quarter, leaf_count, near_index.shape[1], leaf_size)
    near_points = jnp.einsum(
        "lnab,vlnb->vla", near_block, picked, preferred_element_type=jnp.float32
    ).reshape(quarter, -1)
    return (far_mine + near_points).astype(jnp.bfloat16)


def solution(mesh):
    return jax.shard_map(
        body,
        mesh=mesh,
        in_specs=(
            P("cols", "rows"),
            P("rows", None, None),
            P("rows", None, None),
            P("rows", None, None),
            P(),
            P("rows", "cols"),
            P("rows", "cols"),
            P("rows", "cols", None, None),
            P("rows", "cols"),
            P("rows", "cols"),
            P("rows", "cols", None, None),
            P(None, "cols"),
            P(None, "cols", None, None),
            P("rows", None),
            P("rows", None, None, None),
        ),
        out_specs=P("cols", "rows"),
        check_vma=False,
    )
```

profile of v0, /device:TPU:1, one launch (start us, length us, event | category | flops | bytes accessed | tf_op | source)
XLA Modules:
  0.0 365.5 jit_solution(11159115372393035938)
XLA Ops:
  8.8 1.5 reshape.299
  10.3 1.7 convolution_convert_fusion
  12.9 11.2 %all_gather.14 = bf16[8,128,64]{2,1,0:T(8,128)(2,1)S(1)} all-gather(bf16[8,32,64]{2,1,0:T(8,128)(2,1)S(1)} %fusion.22), channel_id=1, replica_groups=mesh['rows'=64,'cols'=4] {'cols'}, dimensions={1}, use_global_device_ids=true | all-gather | bytes 163840 | tf_op jit(solution)/shard_map/all_gather | solution.py:77
  24.6 3.2 gather_fusion.1
  27.9 3.2 gather.39
  31.1 3.3 broadcast_select_fusion.1
  34.4 14.7 %all-to-all-start = ((bf16[64,2,8192]{2,1,0:T(2,128)(2,1)}), bf16[64,2,8192]{2,1,0:T(2,128)(2,1)}, u32[]{:S(2)}, u32[]{:S(2)}) async-start(bf16[64,2,8192]{2,1,0:T(2,128)(2,1)} %broadcast_select_fusion.1), calls=%async_computation | async-start | bytes 4194304 | tf_op jit(solution)/shard_map/all_to_all | solution.py:80
  50.3 35.5 %all-gather.4.cloned.1.call-done = bf16[64,128,64]{2,1,0:T(8,128)(2,1)} async-done(((bf16[64,32,64]{2,1,0:T(8,128)(2,1)}), bf16[64,128,64]{2,1,0:T(8,128)(2,1)}) %all-gather.4.cloned.1.call-update) | async-done | bytes 1048592 | tf_op jit(solution)/shard_map/all_gather | solution.py:64
  85.7 3.3 reshape.313
  89.1 5.1 %gather_fusion.3 = bf16[256,8192]{1,0:T(8,128)(2,1)} fusion(bf16[64,8192]{1,0:T(8,128)(2,1)S(1)} %reshape.313, s32[1024]{0:T(1024)S(1)} %pad_clamp_fusion.2), kind=kCustom, calls=%fused_computation.3 | custom fusion | bytes 8389632 | tf_op jit(solution)/shard_map/jit(_take)/gather | solution.py:32
  94.2 7.2 %gather.43 = bf16[64,4,8192]{2,1,0:T(4,128)(2,1)} reshape(bf16[256,8192]{1,0:T(8,128)(2,1)} %gather_fusion.3) | data formatting | bytes 8388608 | tf_op jit(solution)/shard_map/jit(_take)/gather | solution.py:32
  101.4 6.1 %broadcast_select_fusion = bf16[64,4,8192]{2,1,0:T(4,128)(2,1)} fusion(bf16[64,4,8192]{2,1,0:T(4,128)(2,1)} %gather.43, pred[64,4]{1,0:T(8,128)(4,1)S(1)} %copy.83), kind=kLoop, calls=%fused_computation.13 | loop fusion | flops 2097152 | bytes 8388864 | tf_op jit(solution)/shard_map/jit(_take)/select_n | solution.py:32
  107.6 11.0 %all-to-all-start.1 = ((bf16[64,4,8192]{2,1,0:T(4,128)(2,1)}), bf16[64,4,8192]{2,1,0:T(4,128)(2,1)}, u32[]{:S(2)}, u32[]{:S(2)}) async-start(bf16[64,4,8192]{2,1,0:T(4,128)(2,1)} %broadcast_select_fusion), calls=%async_computation.1 | async-start | bytes 8388608 | tf_op jit(solution)/shard_map/all_to_all | solution.py:65
  118.8 10.5 %all_gather.12 = bf16[128,64]{1,0:T(8,128)(2,1)} all-gather(bf16[32,64]{1,0:T(8,128)(2,1)S(1)} %fusion.23), channel_id=1, replica_groups=mesh['rows'=64,'cols'=4] {'cols'}, dimensions={0}, use_global_device_ids=true | all-gather | bytes 20480 | tf_op jit(solution)/shard_map/all_gather | solution.py:78
  129.7 1.4 slice.17
  131.1 3.3 copy.68
  134.4 2.8 copy.71
  137.5 7.0 %copy.76 = bf16[112,2,64,64]{3,2,1,0:T(8,128)(2,1)} copy(bf16[112,2,64,64]{0,3,2,1:T(8,128)(2,1)} %param.27) | data formatting | bytes 3670016 | tf_op args[12]
  148.3 71.3 %all-gather.6.cloned.1.call-done = bf16[8192,64]{1,0:T(8,128)(2,1)} async-done(((bf16[128,64]{1,0:T(8,128)(2,1)}), bf16[8192,64]{1,0:T(8,128)(2,1)}) %all-gather.6.cloned.1.call-update) | async-done | bytes 1048592 | tf_op jit(solution)/shard_map/all_gather | solution.py:91
  219.6 2.4 fusion.19
  222.0 1.4 copy.73
  224.0 3.6 pad_maximum_fusion
  227.6 10.5 %gather_fusion = bf16[224,128,64]{2,1,0:T(8,128)(2,1)} fusion(bf16[112,128,64]{2,1,0:T(8,128)(2,1)} %pad_maximum_fusion, s32[1024]{0:T(1024)} %pad_clamp_fusion.5), kind=kCustom, calls=%fused_computation | custom fusion | bytes 7340928 | tf_op jit(solution)/shard_map/jit(_take)/gather | solution.py:105
  238.1 8.3 %copy.75 = bf16[224,128,64]{1,2,0:T(8,128)(2,1)} copy(bf16[224,128,64]{2,1,0:T(8,128)(2,1)} %gather_fusion) | data formatting | bytes 7340032 | tf_op jit(solution)/shard_map/jit(_take)/gather | solution.py:105
  246.5 4.6 %fusion.12 = f32[112,128,64]{1,2,0:T(8,128)S(1)} fusion(bf16[112,2,64,64]{3,2,1,0:T(8,128)(2,1)} %copy.76, bf16[112,2,128,64]{2,3,1,0:T(8,128)(2,1)} %bitcast.90, pred[112,2]{1,0:T(8,128)(4,1)S(1)} %copy.65), kind=kOutput, calls=%fused_computation.22 | convolution fusion | flops 236716032 | bytes 9175264 | tf_op jit(solution)/shard_map/ifrs,ifvs->ivr/dot_general | solution.py:107
  252.1 0.8 copy-done.2
  253.1 2.7 fusion.39
  255.9 2.7 all_to_all.13
  258.6 1.8 gather_fusion.2
  260.4 2.9 gather.41
  263.4 1.9 convolution_bitcast_fusion.3
  265.3 1.0 fusion.21
  266.6 1.2 fusion.40
  267.8 6.9 %all_to_all.15 = bf16[256,8192]{1,0:T(8,128)(2,1)} reshape(bf16[64,4,8192]{2,1,0:T(4,128)(2,1)} %all-to-all-done.1) | data formatting | bytes 8388608 | tf_op jit(solution)/shard_map/all_to_all | solution.py:65
  274.6 17.8 %gather_fusion.4 = bf16[384,8192]{1,0:T(8,128)(2,1)} fusion(bf16[256,8192]{1,0:T(8,128)(2,1)} %all_to_all.15, s32[1024]{0:T(1024)S(1)} %copy-done.9), kind=kCustom, calls=%fused_computation.4 | custom fusion | bytes 12584448 | tf_op jit(solution)/shard_map/jit(_take)/gather | solution.py:85
  292.4 17.9 %gather.45 = bf16[64,6,128,64]{3,2,1,0:T(8,128)(2,1)} reshape(bf16[384,8192]{1,0:T(8,128)(2,1)} %gather_fusion.4) | data formatting | bytes 12582912 | tf_op jit(solution)/shard_map/jit(_take)/gather | solution.py:85
  310.3 8.9 %fusion = f32[64,128,64,1]{1,2,3,0:T(8,128)S(1)} fusion(bf16[64,6,64,64]{3,2,1,0:T(8,128)(2,1)} %param.22, bf16[64,6,128,64]{3,2,1,0:T(8,128)(2,1)} %gather.45, pred[64,6]{1,0:T(8,128)(4,1)S(1)} %copy-done.11), kind=kOutput, calls=%fused_computation.6 | convolution fusion | flops 405798912 | bytes 11534720 | tf_op jit(solution)/shard_map/lfrs,lfvs->lvr/dot_general | solution.py:87
  319.2 2.7 fusion.10
  321.9 3.0 copy.87
  324.9 2.1 collective-permute-start
  327.0 2.2 collective-permute-start.1
  330.3 4.4 %collective-permute-done.1 = bf16[32,4096]{1,0:T(8,128)(2,1)S(1)} collective-permute-done((bf16[32,4096]{1,0:T(8,128)(2,1)S(1)}, bf16[32,4096]{1,0:T(8,128)(2,1)S(1)}, u32[]{:S(2)}, u32[]{:S(2)}) %collective-permute-start.1) | collective-permute-done | bytes 262176 | tf_op jit(solution)/shard_map/ppermute | solution.py:17
  334.8 2.9 reshape.317
  337.6 2.4 copy.90
  340.1 3.5 gather_fusion.5
  343.6 6.1 %fusion.16 = f32[32,64,64]{2,0,1:T(8,128)S(1)} fusion(bf16[64,8,64,64]{3,2,1,0:T(8,128)(2,1)} %param.29, bf16[32,64,8,64]{3,0,2,1:T(8,128)(2,1)} %bitcast.89, pred[64,8]{1,0:T(8,128)(4,1)S(1)} %copy.88), kind=kOutput, calls=%fused_computation.24 | convolution fusion | flops 135266304 | bytes 6816256 | tf_op jit(solution)/shard_map/lnab,vlnb->vla/dot_general | solution.py:133
  350.7 5.3 %reduce-scatter.2.cloned.1.call-done = f32[32,4096]{1,0:T(8,128)} async-done(((f32[128,4096]{1,0:T(8,128)}), f32[32,4096]{1,0:T(8,128)}) %reduce-scatter.2.cloned.1.call-update) | async-done | bytes 524304 | tf_op jit(solution)/shard_map/reduce_scatter | solution.py:125
  356.0 1.8 add_convert_fusion
  (93 shorter events, 12.7 us)
Async XLA Ops:
  7.4 4.7 %copy-start = (bf16[64,64,64]{2,1,0:T(8,128)(2,1)S(1)}, bf16[64,64,64]{2,1,0:T(8,128)(2,1)}, u32[]{:S(2)}) copy-start(bf16[64,64,64]{2,1,0:T(8,128)(2,1)} %param.17) | copy-start | bytes 1572868
  12.0 0.8 copy-start.3
  31.1 18.8 %copy-start.12 = (s32[64,4]{0,1:T(4,128)S(1)}, s32[64,4]{0,1:T(4,128)}, u32[]{:S(2)}) copy-start(s32[64,4]{0,1:T(4,128)} %param.20) | copy-start | bytes 3076
  34.4 73.1 %all-to-all-start = ((bf16[64,2,8192]{2,1,0:T(2,128)(2,1)}), bf16[64,2,8192]{2,1,0:T(2,128)(2,1)}, u32[]{:S(2)}, u32[]{:S(2)}) async-start(bf16[64,2,8192]{2,1,0:T(2,128)(2,1)} %broadcast_select_fusion.1), calls=%async_computation | async-start | bytes 4194304 | tf_op jit(solution)/shard_map/all_to_all | solution.py:80
  49.2 36.6 %all-gather.4.cloned.1.call-start = ((), (), s32[]{:S(2)}) async-start(), calls=%async_computation.3 | async-start | bytes 2621440 | tf_op jit(solution)/shard_map/all_gather | solution.py:64
  107.6 11.1 %copy-start.7 = (bf16[8,64,64]{2,1,0:T(8,128)(2,1)S(1)}, bf16[8,64,64]{2,1,0:T(8,128)(2,1)}, u32[]{:S(2)}) copy-start(bf16[8,64,64]{2,1,0:T(8,128)(2,1)} %param.18) | copy-start | bytes 196612
  107.6 22.1 %copy-start.5 = (bf16[96,64,64]{0,2,1:T(8,128)(2,1)S(1)}, bf16[96,64,64]{0,2,1:T(8,128)(2,1)}, u32[]{:S(2)}) copy-start(bf16[96,64,64]{0,2,1:T(8,128)(2,1)} %param.19) | copy-start | bytes 2359300
  107.6 160.2 %all-to-all-start.1 = ((bf16[64,4,8192]{2,1,0:T(4,128)(2,1)}), bf16[64,4,8192]{2,1,0:T(4,128)(2,1)}, u32[]{:S(2)}, u32[]{:S(2)}) async-start(bf16[64,4,8192]{2,1,0:T(4,128)(2,1)} %broadcast_select_fusion), calls=%async_computation.1 | async-start | bytes 8388608 | tf_op jit(solution)/shard_map/all_to_all | solution.py:65
  118.5 18.7 %copy-start.14 = (s32[112,2]{0,1:T(2,128)S(1)}, s32[112,2]{0,1:T(2,128)}, u32[]{:S(2)}) copy-start(s32[112,2]{0,1:T(2,128)} %param.26) | copy-start | bytes 2692
  118.6 101.0 %all-gather.6.cloned.1.call-start = ((), (), s32[]{:S(2)}) async-start(), calls=%async_computation.5 | async-start | bytes 2129920 | tf_op jit(solution)/shard_map/all_gather | solution.py:91
  129.4 226.6 %reduce-scatter.2.cloned.1.call-start = ((), (), s32[]{:S(2)}) async-start(), calls=%async_computation.4 | async-start | bytes 2621440 | tf_op jit(solution)/shard_map/reduce_scatter | solution.py:125
  134.4 10.3 %copy-start.10 = (s32[8,4]{0,1:T(4,128)S(1)}, s32[8,4]{0,1:T(4,128)}, u32[]{:S(2)}) copy-start(s32[8,4]{0,1:T(4,128)} %param.24) | copy-start | bytes 388
  134.4 11.1 %copy-start.8 = (s32[64,6]{0,1:T(8,128)S(1)}, s32[64,6]{0,1:T(8,128)}, u32[]{:S(2)}) copy-start(s32[64,6]{0,1:T(8,128)} %param.21) | copy-start | bytes 4612
  251.1 1.8 copy-start.2
  258.6 4.7 %copy-start.15 = (pred[8,4]{1,0:T(8,128)(4,1)S(1)}, pred[8,4]{1,0:T(8,128)(4,1)}, u32[]{:S(2)}) copy-start(pred[8,4]{1,0:T(8,128)(4,1)} %copy.77) | copy-start | bytes 100
  260.4 4.8 %slice-start = ((f32[112,128,64]{1,2,0:T(8,128)}), f32[64,128,64]{1,2,0:T(8,128)S(1)}, s32[]{:S(2)}) async-start(f32[112,128,64]{1,2,0:T(8,128)} %copy-done.2), calls=%async_computation.6 | async-start | bytes 4194304 | tf_op jit(solution)/shard_map/slice | solution.py:117
  267.7 6.9 %copy-start.9 = (s32[1024]{0:T(1024)S(1)}, s32[1024]{0:T(1024)}, u32[]{:S(2)}) copy-start(s32[1024]{0:T(1024)} %pad_clamp_fusion.1) | copy-start | bytes 12292
  292.4 17.9 %copy-start.11 = (pred[64,6]{1,0:T(8,128)(4,1)S(1)}, pred[64,6]{1,0:T(8,128)(4,1)}, u32[]{:S(2)}) copy-start(pred[64,6]{1,0:T(8,128)(4,1)} %copy.82) | copy-start | bytes 1156
  310.3 8.9 %copy-start.4 = (bf16[64,64,64]{2,1,0:T(8,128)(2,1)S(1)}, bf16[64,64,64]{2,1,0:T(8,128)(2,1)}, u32[]{:S(2)}) copy-start(bf16[64,64,64]{2,1,0:T(8,128)(2,1)} %param.16) | copy-start | bytes 1572868
  321.8 3.0 copy-start.6
  321.8 7.4 %copy-start.13 = (s32[64,8]{0,1:T(8,128)S(1)}, s32[64,8]{0,1:T(8,128)}, u32[]{:S(2)}) copy-start(s32[64,8]{0,1:T(8,128)} %param.28) | copy-start | bytes 6148
  324.9 5.5 %collective-permute-start = (bf16[32,4096]{1,0:T(8,128)(2,1)S(1)}, bf16[32,4096]{1,0:T(8,128)(2,1)S(1)}, u32[]{:S(2)}, u32[]{:S(2)}) collective-permute-start(bf16[32,4096]{1,0:T(8,128)(2,1)S(1)} %copy-done.6), channel_id=1, source_target_pairs={{0,4},{4,8},{8,12},{12,16},{16,20},{20,24},{24,28},{28,32},{32,36}... | collective-permute-start | bytes 786440 | tf_op jit(solution)/shard_map/ppermute | solution.py:14
  327.0 7.7 %collective-permute-start.1 = (bf16[32,4096]{1,0:T(8,128)(2,1)S(1)}, bf16[32,4096]{1,0:T(8,128)(2,1)S(1)}, u32[]{:S(2)}, u32[]{:S(2)}) collective-permute-start(bf16[32,4096]{1,0:T(8,128)(2,1)S(1)} %copy-done.6), channel_id=1, source_target_pairs={{4,0},{8,4},{12,8},{16,12},{20,16},{24,20},{28,24},{32,28},{36,32}... | collective-permute-start | bytes 786440 | tf_op jit(solution)/shard_map/ppermute | solution.py:17
  343.6 14.2 %copy-start.1 = (bf16[64,64,64]{2,1,0:T(8,128)(2,1)S(1)}, bf16[64,64,64]{2,1,0:T(8,128)(2,1)}, u32[]{:S(2)}) copy-start(bf16[64,64,64]{2,1,0:T(8,128)(2,1)} %param.17) | copy-start | bytes 1572868
Sparse Core Ops, SparseCore 0:
  51.8 33.8 all-gather.3
  325.0 30.9 reduce-scatter.1
Sparse Core Ops, SparseCore 1:
  129.4 90.1 all-gather.5
where the time goes:
time: 372 us; the launch traced here: 365 us
  local copies, waits for them, and re-layouts  127 us (34%)
  waiting for transfers between devices  118 us (32%)
  matrix products  34.9 us (9%)
  starting transfers between devices  30.6 us (8%)
  blocking collectives  21.7 us (6%)
  other arithmetic  18.2 us (5%)
  between operations  15.6 us (4%)
    all_gather x1, waiting for transfers between devices, body(): roots_all = lax.all_gather(root_full[None], 'rows', axis=0, tiled=True)  71.3 us
    gather x4, local copies, waits for them, and re-layouts, far_terms(): partner = jnp.take(received, slot_map.reshape(-1), axis=0)  40.4 us
    all_gather x1, waiting for transfers between devices, body(): leaf_full = lax.all_gather(leaf_part, 'cols', axis=1, tiled=True)  35.5 us
    gather x2, local copies, waits for them, and re-layouts, body(): partner = jnp.take(coef_coarse, coarse_far.reshape(-1), axis=0)  18.8 us
    gather x4, local copies, waits for them, and re-layouts, outgoing(): return jnp.take(flat, jnp.maximum(table, 0).reshape(-1), axis=0)  18.7 us
    unnamed x38, local copies, waits for them, and re-layouts  14.8 us
    all_to_all x1, starting transfers between devices, body(): lax.all_to_all(outgoing(box_full, send_box), 'rows', split_axis=0, concat...  14.7 us
    all_gather x1, blocking collectives, body(): lax.all_gather(boxes, 'cols', axis=1, tiled=True)  11.2 us
  transfers between devices with their start and end apart: 7, of which 5 were waited for; matrix products, arithmetic and copies ran while one was open for 28% of the time, Pallas kernels for 0%

commit v1 on v0

v1 whole, which is shorter than its diff:
```python
import jax
import jax.numpy as jnp
from jax import lax
from jax.experimental import pallas as pl
from jax.experimental.pallas import tpu as pltpu
from jax.sharding import PartitionSpec as P

BF = jnp.bfloat16
F32 = jnp.float32
MESH = pl.DeviceIdType.MESH
NX, NZ, NC, NQ = 4, 8, 2, 4
NROWS = NX * NZ * NC
LEAF, BOX, NEAR = 64, 8, 8
FL, FB = 6, 4
TILES = LEAF + BOX + 1
CUT = 36
SLOTS = 7
GROUP = NX * NC * NQ


def rem(a, n):
    return lax.rem(a, n)


def diag(block):
    zero = jnp.zeros_like(block)
    return jnp.concatenate(
        [jnp.concatenate([block, zero], axis=1), jnp.concatenate([zero, block], axis=1)], axis=0
    )


def diag2(first, second):
    zero = jnp.zeros_like(first)
    return jnp.concatenate(
        [jnp.concatenate([first, zero], axis=1), jnp.concatenate([zero, second], axis=1)], axis=0
    )


def dot_nn(a, b):
    return lax.dot_general(a, b, (((1,), (0,)), ((), ())), preferred_element_type=F32)


def dot_nt(a, b):
    return lax.dot_general(a, b, (((1,), (1,)), ((), ())), preferred_element_type=F32)


def split_pair(wide):
    low, high = wide[:16], wide[16:]
    low_turned, high_turned = pltpu.roll(low, 64, 1), pltpu.roll(high, 64, 1)
    first = lax.broadcasted_iota(jnp.int32, (16, 128), 1) < 64
    return jnp.where(first, low, high_turned), jnp.where(first, low_turned, high)


def join_pair(even, odd):
    even_turned, odd_turned = pltpu.roll(even, 64, 1), pltpu.roll(odd, 64, 1)
    first = lax.broadcasted_iota(jnp.int32, (16, 128), 1) < 64
    return jnp.concatenate(
        [jnp.where(first, even, odd_turned), jnp.where(first, even_turned, odd)], axis=0
    )


def exchange_kernel(
    points, basis, leaf_transfer, box_transfer, table,
    recv, near,
    *scratch,
):
    held, scratch = scratch[:NZ], scratch[NZ:]
    tables, staged, own_points, index = scratch[:4]
    (
        tab_send, tab_recv, ring_send, ring_recv, out_send, out_recv, self_sem,
        near_send, near_recv, near_self, index_sem,
    ) = scratch[4:]
    mine = held[0]
    me, v = lax.axis_index("rows"), lax.axis_index("cols")
    c = rem(me, NC)
    z = rem(me // NC, NZ)
    x = me // (NC * NZ)

    def row(xx, zz, cc):
        return (xx * NZ + zz) * NC + cc

    def target(k):
        dx, dc, dq = k // (NC * NQ), rem(k // NQ, NC), rem(k, NQ)
        return row(rem(x + dx, NX), z, rem(c + dc, NC)), rem(v + dq, NQ), dq

    z_up, z_down = row(x, rem(z + 1, NZ), c), row(x, rem(z + NZ - 1, NZ), c)
    far_side = rem(me + 2 * c - 1 + NROWS, NROWS)
    barrier = pltpu.get_barrier_semaphore()

    @pl.loop(1, GROUP)
    def _(k):
        d, q, _ = target(k)
        pl.semaphore_signal(barrier, inc=1, device_id=(d, q), device_id_type=MESH)

    for d in (z_up, z_down, far_side):
        pl.semaphore_signal(barrier, inc=1, device_id=(d, v), device_id_type=MESH)
    tables[0, 0] = table[...]
    pl.semaphore_wait(barrier, GROUP + 2)

    for step in range(1, NQ):
        pltpu.make_async_remote_copy(
            src_ref=table, dst_ref=tables.at[0, NQ - step],
            send_sem=tab_send, recv_sem=tab_recv,
            device_id=(me, rem(v + step, NQ)), device_id_type=MESH,
        ).start()

    @pl.loop(0, BOX)
    def _(k):
        pairs = []
        for j in range(4):
            pair = k * 4 + j
            block = points[:, pl.ds(pl.multiple_of(pair * 128, 128), 128)]
            even, odd = split_pair(block.astype(F32))
            own_points[2 * pair] = even.astype(BF)
            own_points[2 * pair + 1] = odd.astype(BF)
            coef = dot_nn(block, diag2(basis[2 * pair], basis[2 * pair + 1]))
            pairs.append(coef.astype(BF))
            even, odd = split_pair(coef)
            mine[2 * pair] = even.astype(BF)
            mine[2 * pair + 1] = odd.astype(BF)
        wide = jnp.concatenate(pairs, axis=1)
        box = dot_nn(wide, leaf_transfer[pl.ds(k * 8, 8)].reshape(512, 64))
        mine[LEAF + k] = jnp.concatenate([box[:16], box[16:]], axis=1).astype(BF)

    first = lax.broadcasted_iota(jnp.int32, (16, 128), 1) < 64
    total = jnp.zeros((32, 64), F32)
    for k in range(BOX):
        tile = mine[LEAF + k].astype(F32)
        low = tile[:, :64]
        high = pltpu.roll(tile, 64, 1)[:, :64]
        total += dot_nn(jnp.concatenate([low, high], axis=0).astype(BF), box_transfer[k])
    mine[LEAF + BOX] = jnp.concatenate([total[:16], total[16:]], axis=1).astype(BF)

    pltpu.make_async_copy(tables.at[0, pl.ds(1, NQ - 1)], tables.at[0, pl.ds(1, NQ - 1)], tab_recv).wait()
    pltpu.make_async_copy(tables.at[0, pl.ds(1, NQ - 1)], tables.at[0, pl.ds(1, NQ - 1)], tab_send).wait()

    def ring(way, step, piece):
        if way == 0:
            src, dst, to = (NZ - step + 1) % NZ, NZ - step, z_up
        else:
            src, dst, to = step - 1, step, z_down
        if piece == 2:
            src_ref, dst_ref = tables.at[src], tables.at[dst]
        else:
            part = pl.ds(0, CUT) if piece == 0 else pl.ds(CUT, TILES - CUT)
            src_ref, dst_ref = held[src].at[part], held[dst].at[part]
        return pltpu.make_async_remote_copy(
            src_ref=src_ref, dst_ref=dst_ref,
            send_sem=ring_send.at[way, step - 1, piece], recv_sem=ring_recv.at[dst, piece],
            device_id=(to, v), device_id_type=MESH,
        )

    def parts(step):
        if step < NZ // 2:
            return [(way, piece) for piece in (2, 0, 1) for way in (0, 1)]
        return [(0, 2), (0, 0), (1, 1)]

    for way, piece in parts(1):
        ring(way, 1, piece).start()

    near_up = pltpu.make_async_remote_copy(
        src_ref=own_points, dst_ref=near.at[0], send_sem=near_send.at[0], recv_sem=near_recv.at[0],
        device_id=(rem(me + 1, NROWS), v), device_id_type=MESH,
    )
    near_down = pltpu.make_async_remote_copy(
        src_ref=own_points, dst_ref=near.at[2], send_sem=near_send.at[1], recv_sem=near_recv.at[1],
        device_id=(rem(me + NROWS - 1, NROWS), v), device_id_type=MESH,
    )
    near_here = pltpu.make_async_copy(own_points, near.at[1], near_self)

    def pack(off):
        fetch = pltpu.make_async_copy(tables.at[off], index.at[off], index_sem)
        fetch.start()
        fetch.wait()
        source = row(x, rem(z + off, NZ), c)

        def fill(k):
            d, q, dq = target(k)
            hi, lo = d // 8, rem(d, 8) * 16
            for j in range(SLOTS - 1):
                tile = jnp.maximum(index[off, dq, hi, lo + j], 0)
                if j >= 4:
                    tile = tile + LEAF
                staged[k, off, j] = held[off][tile]
            staged[k, off, SLOTS - 1] = held[off][LEAF + BOX]
            return d, q

        @pl.loop(1, GROUP)
        def _(k):
            d, q = fill(k)
            pltpu.make_async_remote_copy(
                src_ref=staged.at[k, off], dst_ref=recv.at[v, source],
                send_sem=out_send, recv_sem=out_recv, device_id=(d, q), device_id_type=MESH,
            ).start()

        fill(0)
        pltpu.make_async_copy(staged.at[0, off], recv.at[v, source], self_sem).start()

    pack(0)
    near_up.start()
    near_down.start()
    near_here.start()
    for step in range(1, NZ // 2 + 1):
        for way, piece in parts(step):
            ring(way, step, piece).wait_recv()
            if (way, piece) in parts(step + 1) and step < NZ // 2:
                ring(way, step + 1, piece).start()
        pack(NZ - step)
        if step < NZ // 2:
            pack(step)

    for step in range(1, NZ // 2 + 1):
        for way, piece in parts(step):
            ring(way, step, piece).wait_send()
    others = staged.at[pl.ds(1, GROUP - 1)]
    pltpu.make_async_copy(others, others, out_send).wait()
    pltpu.make_async_copy(others, others, out_recv).wait()
    pltpu.make_async_copy(staged.at[0], staged.at[0], self_sem).wait()
    near_here.wait()
    near_up.wait()
    near_down.wait()


def exchange(points, basis, leaf_transfer, box_transfer, table):
    return pl.pallas_call(
        exchange_kernel,
        out_shape=(
            jax.ShapeDtypeStruct((NQ, NROWS, SLOTS, 16, 128), BF),
            jax.ShapeDtypeStruct((3, LEAF, 16, 128), BF),
        ),
        in_specs=[pl.BlockSpec(memory_space=pltpu.VMEM)] * 5,
        out_specs=(pl.BlockSpec(memory_space=pl.ANY), pl.BlockSpec(memory_space=pl.ANY)),
        scratch_shapes=[
            *[pltpu.VMEM((TILES, 16, 128), BF)] * NZ,
            pltpu.VMEM((NZ, NQ, 8, 128), jnp.int32),
            pltpu.VMEM((GROUP, NZ, SLOTS, 16, 128), BF),
            pltpu.VMEM((LEAF, 16, 128), BF),
            pltpu.SMEM((NZ, NQ, 8, 128), jnp.int32),
            pltpu.SemaphoreType.DMA,
            pltpu.SemaphoreType.DMA,
            pltpu.SemaphoreType.DMA((2, NZ // 2, 3)),
            pltpu.SemaphoreType.DMA((NZ, 3)),
            pltpu.SemaphoreType.DMA,
            pltpu.SemaphoreType.DMA,
            pltpu.SemaphoreType.DMA,
            pltpu.SemaphoreType.DMA((2,)),
            pltpu.SemaphoreType.DMA((2,)),
            pltpu.SemaphoreType.DMA,
            pltpu.SemaphoreType.DMA,
        ],
        compiler_params=pltpu.CompilerParams(
            collective_id=0, has_side_effects=True, vmem_limit_bytes=48 * 2**20
        ),
        name="exchange",
    )(points, basis, leaf_transfer, box_transfer, table)


def far_kernel(
    place, leaf_far, box_far, coarse_far,
    recv, leaf_coupling, box_coupling, coarse_coupling, leaf_transfer, box_transfer, coarse_transfer,
    out, root_field, coarse_blocks, sems,
):
    step = pl.program_id(0)
    d = place[0]

    def slot(p, j):
        return recv[:, p, j].reshape(64, 128)

    @pl.when(step == 0)
    def _():
        nodes = (d // 4, NROWS // 4 + d // 2, 3 * NROWS // 4 + d)
        copies = [
            pltpu.make_async_copy(coarse_coupling.at[n], coarse_blocks.at[i], sems.at[i])
            for i, n in enumerate(nodes)
        ]
        for copy in copies:
            copy.start()
        half = NROWS // 2

        def root(n):
            return slot(n, SLOTS - 1)

        def mid(n):
            both = dot_nn(root(2 * n), diag(coarse_transfer[half + 2 * n]))
            both += dot_nn(root(2 * n + 1), diag(coarse_transfer[half + 2 * n + 1]))
            return both.astype(BF)

        def top(n):
            both = dot_nn(mid(2 * n), diag(coarse_transfer[2 * n]))
            both += dot_nn(mid(2 * n + 1), diag(coarse_transfer[2 * n + 1]))
            return both.astype(BF)

        for copy in copies:
            copy.wait()
        field = jnp.zeros((64, 128), F32)
        starts = (0, NROWS // 4, 3 * NROWS // 4)
        for level, make in enumerate((top, mid, root)):
            if level == 1:
                field = dot_nt(field.astype(BF), diag(coarse_transfer[d // 2]))
            if level == 2:
                field = dot_nt(field.astype(BF), diag(coarse_transfer[half + d]))
            for e in range(2):
                partner = coarse_far[nodes[level], e] - starts[level]
                field += dot_nt(make(partner), diag(coarse_blocks[level, e]))
        root_field[...] = field.astype(BF)

    box = dot_nt(root_field[...], diag(box_transfer[0]))
    for e in range(FB):
        entry = box_far[step, e]
        box += dot_nt(slot(entry // 2, 4 + rem(entry, 2)), diag(box_coupling[0, e]))
    box = box.astype(BF)

    for l in range(8):
        left, right = [box], [diag(leaf_transfer[l])]
        for e in range(FL):
            entry = leaf_far[step * 8 + l, e]
            left.append(slot(entry // 4, rem(entry, 4)))
            right.append(diag(leaf_coupling[l, e]))
        field = dot_nt(jnp.concatenate(left, axis=1), jnp.concatenate(right, axis=1))
        out[:, l] = field.astype(BF).reshape(NQ, 16, 128)


def far(place, leaf_far, box_far, coarse_far, recv, leaf_coupling, box_coupling, coarse_coupling,
        leaf_transfer, box_transfer, coarse_transfer):
    whole = pl.BlockSpec(memory_space=pltpu.VMEM)
    return pl.pallas_call(
        far_kernel,
        out_shape=jax.ShapeDtypeStruct((NQ, LEAF, 16, 128), BF),
        grid_spec=pltpu.PrefetchScalarGridSpec(
            num_scalar_prefetch=4,
            grid=(BOX,),
            in_specs=[
                whole,
                pl.BlockSpec((8, FL, 64, 64), lambda i, *_: (i, 0, 0, 0)),
                pl.BlockSpec((1, FB, 64, 64), lambda i, *_: (i, 0, 0, 0)),
                pl.BlockSpec(memory_space=pl.ANY),
                pl.BlockSpec((8, 64, 64), lambda i, *_: (i, 0, 0)),
                pl.BlockSpec((1, 64, 64), lambda i, *_: (i, 0, 0)),
                whole,
            ],
            out_specs=pl.BlockSpec((NQ, 8, 16, 128), lambda i, *_: (0, i, 0, 0)),
            scratch_shapes=[
                pltpu.VMEM((64, 128), BF),
                pltpu.VMEM((3, 2, 64, 64), BF),
                pltpu.SemaphoreType.DMA((3,)),
            ],
        ),
        compiler_params=pltpu.CompilerParams(vmem_limit_bytes=48 * 2**20),
        name="far",
    )(place, leaf_far, box_far, coarse_far, recv, leaf_coupling, box_coupling, coarse_coupling,
      leaf_transfer, box_transfer, coarse_transfer)


def finish_kernel(near_index, partial, near, near_block, basis, out, arrived, near_sum, send_sem, recv_sem):
    me, v = lax.axis_index("rows"), lax.axis_index("cols")
    barrier = pltpu.get_barrier_semaphore()
    for step in range(1, NQ):
        pl.semaphore_signal(
            barrier, inc=1, device_id=(me, rem(v + step, NQ)), device_id_type=MESH
        )
    pl.semaphore_wait(barrier, NQ - 1)
    copies = []
    for step in range(1, NQ):
        q = rem(v + step, NQ)
        copy = pltpu.make_async_remote_copy(
            src_ref=partial.at[q], dst_ref=arrived.at[step - 1],
            send_sem=send_sem.at[step - 1], recv_sem=recv_sem.at[step - 1],
            device_id=(me, q), device_id_type=MESH,
        )
        copy.start()
        copies.append(copy)

    @pl.loop(0, LEAF)
    def _(l):
        left = [near[near_index[l, n]] for n in range(NEAR)]
        right = [diag(near_block[l, n]) for n in range(NEAR)]
        near_sum[l] = dot_nt(jnp.concatenate(left, axis=1), jnp.concatenate(right, axis=1))

    for copy in copies:
        copy.wait()

    @pl.loop(0, LEAF // 2)
    def _(j):
        pair = []
        for t in range(2):
            l = 2 * j + t
            field = partial[v, l].astype(F32)
            for step in range(NQ - 1):
                field += arrived[step, l].astype(F32)
            pair.append(dot_nt(field.astype(BF), diag(basis[l])) + near_sum[l])
        out[:, pl.ds(pl.multiple_of(j * 128, 128), 128)] = join_pair(*pair).astype(BF)


def finish(near_index, partial, near, near_block, basis):
    vmem = pl.BlockSpec(memory_space=pltpu.VMEM)
    return pl.pallas_call(
        finish_kernel,
        out_shape=jax.ShapeDtypeStruct((32, LEAF * 64), BF),
        in_specs=[pl.BlockSpec(memory_space=pltpu.SMEM)] + [vmem] * 4,
        out_specs=vmem,
        scratch_shapes=[
            pltpu.VMEM((NQ - 1, LEAF, 16, 128), BF),
            pltpu.VMEM((LEAF, 16, 128), F32),
            pltpu.SemaphoreType.DMA((NQ - 1,)),
            pltpu.SemaphoreType.DMA((NQ - 1,)),
        ],
        compiler_params=pltpu.CompilerParams(
            collective_id=1, has_side_effects=True, vmem_limit_bytes=48 * 2**20
        ),
        name="finish",
    )(near_index, partial, near, near_block, basis)


def body(
    points, basis, leaf_transfer, box_transfer, coarse_transfer, send_leaf, leaf_far, leaf_coupling,
    send_box, box_far, box_coupling, coarse_far, coarse_coupling, near_index, near_block,
):
    me = lax.axis_index("rows")
    table = jnp.concatenate(
        [send_leaf, send_box, jnp.zeros((NROWS, 10), jnp.int32)], axis=1
    ).reshape(8, 128)
    recv, near = exchange(points, basis, leaf_transfer, box_transfer, table)
    partial = far(
        jnp.full((1,), me, jnp.int32), leaf_far, box_far, coarse_far, recv, leaf_coupling,
        box_coupling, coarse_coupling, leaf_transfer, box_transfer, coarse_transfer,
    )
    local = jnp.clip(near_index - (me - 1) * LEAF, 0, 3 * LEAF - 1)
    return finish(local, partial, near.reshape(3 * LEAF, 16, 128), near_block, basis)


def solution(mesh):
    return jax.shard_map(
        body,
        mesh=mesh,
        in_specs=(
            P("cols", "rows"),
            P("rows", None, None),
            P("rows", None, None),
            P("rows", None, None),
            P(),
            P("rows", "cols"),
            P("rows", "cols"),
            P("rows", "cols", None, None),
            P("rows", "cols"),
            P("rows", "cols"),
            P("rows", "cols", None, None),
            P(None, "cols"),
            P(None, "cols", None, None),
            P("rows", None),
            P("rows", None, None, None),
        ),
        out_specs=P("cols", "rows"),
        check_vma=False,
    )
```

time: 372 us -> 170 us (0.46); the launches traced: 365 us -> 170 us
  Pallas kernels: 0 us -> 145 us
  waiting for transfers between devices: 118 us -> 0 us
  local copies, waits for them, and re-layouts: 127 us -> 23.2 us
  matrix products: 34.9 us -> 0 us
  starting transfers between devices: 30.6 us -> 0 us
  blocking collectives: 21.7 us -> 0 us
  other arithmetic: 18.2 us -> 0.78 us
  between operations: 15.6 us -> 0.09 us
    pallas_call x0 -> x3, Pallas kernels: none -> 145 us  [the longest x1 101 us: exchange(): pl.pallas_call(exchange_kernel, out_shape=(jax.ShapeDtypeStruct((NQ, NROW...]
    all_gather x2 -> x0, waiting for transfers between devices: 107 us -> none  [the longest x1 71.3 us: body(): roots_all = lax.all_gather(root_full[None], 'rows', axis=0, tiled=True)]
    gather x11 -> x0, local copies, waits for them, and re-layouts: 81.5 us -> none  [the longest x4 40.4 us: far_terms(): partner = jnp.take(received, slot_map.reshape(-1), axis=0)]
    dot_general x14 -> x0, matrix products: 34.9 us -> none  [the longest x2 10.8 us: far_terms(): jnp.einsum('lfrs,lfvs->lvr', coupling, partner, preferred_element_type=jn...]
    all_to_all x2 -> x0, starting transfers between devices: 25.7 us -> none  [the longest x1 14.7 us: body(): lax.all_to_all(outgoing(box_full, send_box), 'rows', split_axis=0, concat...]
    all_gather x2 -> x0, blocking collectives: 21.7 us -> none  [the longest x1 11.2 us: body(): lax.all_gather(boxes, 'cols', axis=1, tiled=True)]
    reshape x13 -> x1, local copies, waits for them, and re-layouts: 14.4 us -> 0.08 us  [body(): table = jnp.concatenate([send_leaf, send_box, jnp.zeros((NROWS, 10), jnp....]
    all_to_all x2 -> x0, local copies, waits for them, and re-layouts: 9.62 us -> none  [the longest x1 6.88 us: body(): lax.all_to_all(outgoing(leaf_full, send_leaf), 'rows', split_axis=0, conc...]
  transfers between devices with their start and end apart: 7 -> 0, of which waited for: 5 -> 0; matrix products, arithmetic and copies ran while one was open for 28% -> 0% of each run, Pallas kernels for 0% -> 0%
where the time goes in v1:
time: 170 us
  Pallas kernels  145 us (85%)
  local copies, waits for them, and re-layouts  23.2 us (14%)
    pallas_call x1, Pallas kernels, exchange(): pl.pallas_call(exchange_kernel, out_shape=(jax.ShapeDtypeStruct((NQ, NROW...  101 us
    pallas_call x1, Pallas kernels, finish(): pl.pallas_call(finish_kernel, out_shape=jax.ShapeDtypeStruct((32, LEAF *...  28.7 us
    unnamed x38, local copies, waits for them, and re-layouts  22.9 us
    pallas_call x1, Pallas kernels, far(): pl.pallas_call(far_kernel, out_shape=jax.ShapeDtypeStruct((NQ, LEAF, 16,...  16.3 us

profile of v1, /device:TPU:1, one launch (start us, length us, event | category | flops | bytes accessed | tf_op | source)
XLA Modules:
  0.0 169.5 jit_solution(5740598547627766119)
XLA Ops:
  0.0 0.0 copy-start.15
  0.0 0.0 copy-start.12
  0.0 0.0 copy-start.14
  0.0 0.1 pad.2.clone
  0.1 0.8 add_add_fusion
  0.9 0.1 copy.44
  1.0 0.1 reshape.6.table
  1.0 0.0 copy-start
  1.0 1.2 copy-done
  2.3 0.0 copy-start.2
  2.3 1.2 copy-done.2
  3.5 0.0 copy-start.6
  3.5 0.9 copy-done.6
  4.4 0.0 copy-start.9
  4.4 0.9 copy-done.9
  5.3 0.0 copy-start.1
  5.3 0.0 copy-start.7
  5.3 100.5 %exchange.1 = (bf16[4,64,7,16,128]{4,3,2,1,0:T(8,128)(2,1)}, bf16[3,64,16,128]{3,2,1,0:T(8,128)(2,1)S(1)}) custom-call(bf16[32,4096]{1,0:T(8,128)(2,1)S(1)} %copy-done.9, bf16[64,64,64]{2,1,0:T(8,128)(2,1)S(1)} %copy-done.2, bf16[64,64,64]{2,1,0:T(8,128)(2,1)S(1)} %copy-done, bf16[8,64,64]{2,1,0:T(8,128)(2,1)S(1)} %copy-done.6, s32[8,128]{1,0:T(8,128)S(1)} %reshape.6.table), custom_call_target="tpu_custom_call" | custom-call | tf_op jit(solution)/shard_map/exchange/pallas_call | solution.py:225
  105.9 7.0 %copy.48.coarse_coupling = bf16[112,2,64,64]{3,2,1,0:T(8,128)(2,1)} copy(bf16[112,2,64,64]{0,3,2,1:T(8,128)(2,1)} %param.27) | data formatting | bytes 3670016 | tf_op args[12]
  112.9 3.3 %copy.49.coarse_transfer = bf16[96,64,64]{2,1,0:T(8,128)(2,1)S(1)} copy(bf16[96,64,64]{0,2,1:T(8,128)(2,1)} %param.19) | data formatting | bytes 1572864 | tf_op args[4]
  116.2 0.0 copy-done.15
  116.2 0.7 copy.47.coarse_far
  116.9 0.0 copy-done.12
  116.9 0.7 copy.45.leaf_far
  117.6 0.0 copy-done.14
  117.6 0.1 copy.46.box_far
  117.7 0.0 copy-done.1
  117.7 0.0 copy-done.7
  117.7 0.0 copy-start.8
  117.7 1.0 copy-done.8
  118.8 0.0 copy-start.10
  118.8 0.8 copy-done.10
  119.6 0.0 copy-start.11
  119.6 0.8 copy-done.11
  120.3 0.0 copy-start.13
  120.3 16.3 %far.1.partial = bf16[4,64,16,128]{3,2,1,0:T(8,128)(2,1)S(1)} custom-call(s32[1]{0:T(128)} %bitcast.place, s32[64,6]{1,0:T(8,128)S(1)} %copy-done.11, s32[8,4]{1,0:T(8,128)S(1)} %copy.46.box_far, s32[112,2]{1,0:T(8,128)S(1)} %copy-done.10, bf16[4,64,7,16,128]{4,3,2,1,0:T(8,128)(2,1)} %get-tuple-element.7.recv, bf16[64,6,64,64]{3,2,1,0:T(8,128)(2,1)} %leaf_coupling.1, ...), custom_call_target="tpu_custom_call" | custom-call | tf_op jit(solution)/shard_map/far/pallas_call | solution.py:326
  136.6 0.0 copy-start.4
  136.7 1.0 copy-done.4
  137.6 0.0 copy-done.13
  137.6 0.1 copy.43
  137.7 0.0 copy-start.3
  137.7 1.2 copy-done.3
  139.0 0.0 copy-start.5
  139.0 1.2 copy-done.5
  140.2 28.7 %finish.1 = bf16[32,4096]{1,0:T(8,128)(2,1)S(1)} custom-call(s32[64,8]{1,0:T(8,128)S(1)} %broadcast_clamp_fusion.near_index, bf16[4,64,16,128]{3,2,1,0:T(8,128)(2,1)S(1)} %copy-done.5, bf16[192,16,128]{2,1,0:T(8,128)(2,1)S(1)} %bitcast.2, bf16[64,8,64,64]{3,2,1,0:T(8,128)(2,1)} %near_block.1, bf16[64,64,64]{2,1,0:T(8,128)(2,1)S(1)} %copy-done.3), custom_call_target="tpu_custom_call" | custom-call | tf_op jit(solution)/shard_map/finish/pallas_call | solution.py:396
  168.8 0.7 copy.51
  (3 shorter events, 0.0 us)
Async XLA Ops:
  0.0 116.2 %copy-start.15 = (s32[112,2]{0,1:T(2,128)S(1)}, s32[112,2]{0,1:T(2,128)}, u32[]{:S(2)}) copy-start(s32[112,2]{0,1:T(2,128)} %param.26) | copy-start | bytes 2692
  0.0 116.9 %copy-start.12 = (s32[64,6]{0,1:T(8,128)S(1)}, s32[64,6]{0,1:T(8,128)}, u32[]{:S(2)}) copy-start(s32[64,6]{0,1:T(8,128)} %param.21) | copy-start | bytes 4612
  0.0 117.6 %copy-start.14 = (s32[8,4]{0,1:T(4,128)S(1)}, s32[8,4]{0,1:T(4,128)}, u32[]{:S(2)}) copy-start(s32[8,4]{0,1:T(4,128)} %param.24) | copy-start | bytes 388
  1.0 1.2 copy-start
  2.3 1.2 copy-start.2
  3.5 0.9 copy-start.6
  4.4 0.9 copy-start.9
  5.3 112.4 %copy-start.1 = (bf16[64,64,64]{2,1,0:T(8,128)(2,1)S(1)}, bf16[64,64,64]{2,1,0:T(8,128)(2,1)}, u32[]{:S(2)}) copy-start(bf16[64,64,64]{2,1,0:T(8,128)(2,1)} %leaf_transfer.3) | copy-start | bytes 1572868
  5.3 112.4 %copy-start.7 = (bf16[8,64,64]{2,1,0:T(8,128)(2,1)S(1)}, bf16[8,64,64]{2,1,0:T(8,128)(2,1)}, u32[]{:S(2)}) copy-start(bf16[8,64,64]{2,1,0:T(8,128)(2,1)} %box_transfer.3) | copy-start | bytes 196612
  117.7 1.0 copy-start.8
  118.8 0.8 copy-start.10
  119.6 0.8 copy-start.11
  120.3 17.3 %copy-start.13 = (s32[64,8]{0,1:T(8,128)S(1)}, s32[64,8]{0,1:T(8,128)}, u32[]{:S(2)}) copy-start(s32[64,8]{0,1:T(8,128)} %param.28) | copy-start | bytes 6148
  136.6 1.0 copy-start.4
  137.7 1.2 copy-start.3
  139.0 1.2 copy-start.5

commit v2 on v0

v2 whole, which is shorter than its diff:
```python
import jax
import jax.numpy as jnp
from jax import lax
from jax.experimental import pallas as pl
from jax.experimental.pallas import tpu as pltpu
from jax.sharding import PartitionSpec as P

BF = jnp.bfloat16
F32 = jnp.float32
I32 = jnp.int32
MESH = pl.DeviceIdType.MESH
NX, NZ, NC, NQ = 4, 8, 2, 4
NROWS = NX * NZ * NC
LEAF, BOX, NEAR = 64, 8, 8
FL, FB = 6, 4
TILES = LEAF + BOX + 1
TOP = BOX + 1
SLOTS = 4
GROUP = NX * NC * NQ
CHUNK = 16


def rem(a, n):
    return lax.rem(a, n)


def side(a, b):
    return jnp.concatenate([a, b], axis=1)


def diag(first, second):
    zero = jnp.zeros_like(first)
    return jnp.concatenate([side(first, zero), side(zero, second)], axis=0)


def dot_nn(a, b):
    return lax.dot_general(a, b, (((1,), (0,)), ((), ())), preferred_element_type=F32)


def dot_nt(a, b):
    return lax.dot_general(a, b, (((1,), (1,)), ((), ())), preferred_element_type=F32)


def split_pair(wide):
    low, high = wide[:16], wide[16:]
    low_turned, high_turned = pltpu.roll(low, 64, 1), pltpu.roll(high, 64, 1)
    first = lax.broadcasted_iota(I32, (16, 128), 1) < 64
    return jnp.where(first, low, high_turned), jnp.where(first, low_turned, high)


def join_pair(even, odd):
    even_turned, odd_turned = pltpu.roll(even, 64, 1), pltpu.roll(odd, 64, 1)
    first = lax.broadcasted_iota(I32, (16, 128), 1) < 64
    return jnp.concatenate(
        [jnp.where(first, even, odd_turned), jnp.where(first, even_turned, odd)], axis=0
    )


def join_tiles(even, odd):
    return join_pair(even.astype(F32), odd.astype(F32)).astype(BF)


def kernel(
    points, ints, basis_h, leaf_h, box_h, leaf_coupling, box_coupling, coarse_h, coarse_coupling,
    near_block, out, *scratch,
):
    held, scratch = scratch[:NZ], scratch[NZ:]
    (
        tables, index, lists, lists_s, ints_s, staged, recv, every, rows_out, rows_in, rows_s,
        near, near_pair, base_pair, basis_pair, weights,
        basis, leaf_transfer, box_transfer, box_raw, coarse_raw, coupling_raw, near_raw, leaf_raw,
        coarse, picked, shared, upper, part, arrived,
    ) = scratch[:30]
    (
        load, chunk_load, tab_send, tab_recv, ring_send, ring_recv, out_send, out_recv, self_sem,
        near_send, near_recv, index_sem, every_send, every_recv, every_self, sibling_recv,
        rows_send, rows_recv, shared_send, shared_recv, part_send, part_recv,
    ) = scratch[30:]
    mine = held[0]
    me, v = lax.axis_index("rows"), lax.axis_index("cols")
    c = rem(me, NC)
    z = rem(me // NC, NZ)
    x = me // (NC * NZ)

    def row(xx, zz, cc):
        return (xx * NZ + zz) * NC + cc

    def target(k):
        dx, dc, dq = k // (NC * NQ), rem(k // NQ, NC), rem(k, NQ)
        return row(rem(x + dx, NX), z, rem(c + dc, NC)), rem(v + dq, NQ), dq

    def remote(src, dst, send, arrive, d, q):
        return pltpu.make_async_remote_copy(
            src_ref=src, dst_ref=dst, send_sem=send, recv_sem=arrive,
            device_id=(d, q), device_id_type=MESH,
        )

    def settle(ref, sem):
        pltpu.make_async_copy(ref, ref, sem).wait()

    loads = [
        pltpu.make_async_copy(src, dst, load.at[i])
        for i, (src, dst) in enumerate((
            (basis_h, basis), (leaf_h, leaf_transfer), (box_h, box_transfer),
            (ints.at[pl.ds(16, 8)], ints_s), (box_coupling, box_raw),
            (coarse_coupling, coupling_raw), (coarse_h, coarse_raw),
        ))
    ]
    for copy in loads:
        copy.start()

    def chunk_copies(i):
        part_of = pl.ds(i * CHUNK, CHUNK)
        return (
            pltpu.make_async_copy(near_block.at[part_of], near_raw.at[i % 2], chunk_load.at[0, i % 2]),
            pltpu.make_async_copy(leaf_coupling.at[part_of], leaf_raw.at[i % 2], chunk_load.at[1, i % 2]),
        )

    z_up, z_down = row(x, rem(z + 1, NZ), c), row(x, rem(z + NZ - 1, NZ), c)
    sibling = row(x, z, 1 - c)
    far_side = rem(me + 2 * c - 1 + NROWS, NROWS)
    barrier = pltpu.get_barrier_semaphore()

    @pl.loop(1, GROUP)
    def _(k):
        d, q, _ = target(k)
        pl.semaphore_signal(barrier, inc=1, device_id=(d, q), device_id_type=MESH)

    for d in (z_up, z_down, far_side):
        pl.semaphore_signal(barrier, inc=1, device_id=(d, v), device_id_type=MESH)
    tables[0, 0] = ints[pl.ds(0, 8)]
    lists[0] = ints[pl.ds(8, 8)]

    @pl.loop(0, LEAF // 2)
    def _(j):
        block = points[:, pl.ds(pl.multiple_of(j * 128, 128), 128)]
        even, odd = split_pair(block.astype(F32))
        near[LEAF + 2 * j] = even.astype(BF)
        near[LEAF + 2 * j + 1] = odd.astype(BF)

    pl.semaphore_wait(barrier, GROUP + 2)

    for step in range(1, NQ):
        q = rem(v + step, NQ)
        remote(ints.at[pl.ds(0, 8)], tables.at[0, NQ - step], tab_send.at[0], tab_recv.at[0], me, q).start()
        remote(ints.at[pl.ds(8, 8)], lists.at[NQ - step], tab_send.at[1], tab_recv.at[1], me, q).start()
    own_near = near.at[pl.ds(LEAF, LEAF)]
    near_copies = (
        remote(own_near, near.at[pl.ds(0, LEAF)], near_send.at[0], near_recv.at[0], rem(me + 1, NROWS), v),
        remote(own_near, near.at[pl.ds(2 * LEAF, LEAF)], near_send.at[1], near_recv.at[1], rem(me + NROWS - 1, NROWS), v),
    )

    loads[0].wait()
    loads[1].wait()
    loads[2].wait()

    def coefficients(k):
        for j in range(4):
            pair = k * 4 + j
            block = points[:, pl.ds(pl.multiple_of(pair * 128, 128), 128)]
            wide = diag(basis[2 * pair], basis[2 * pair + 1])
            basis_pair[pair] = wide
            coef = dot_nn(block, wide)
            near_pair[pair] = coef
            even, odd = split_pair(coef)
            mine[2 * pair] = even.astype(BF)
            mine[2 * pair + 1] = odd.astype(BF)

    pl.loop(0, BOX)(coefficients)

    settle(tables.at[0, pl.ds(1, NQ - 1)], tab_recv.at[0])

    PIECES = {0: pl.ds(0, 32), 1: pl.ds(32, 32), 3: pl.ds(LEAF, TOP)}

    def ring(way, step, piece):
        if way == 0:
            src, dst, to = (NZ - step + 1) % NZ, NZ - step, z_up
        else:
            src, dst, to = step - 1, step, z_down
        if piece == 2:
            src_ref, dst_ref = tables.at[src], tables.at[dst]
        else:
            src_ref, dst_ref = held[src].at[PIECES[piece]], held[dst].at[PIECES[piece]]
        return remote(
            src_ref, dst_ref, ring_send.at[way, step - 1, piece], ring_recv.at[dst, piece], to, v
        )

    def parts(step):
        if step < NZ // 2:
            return [(way, piece) for piece in (2, 0, 1, 3) for way in (0, 1)]
        return [(0, 2), (0, 0), (1, 1), (1, 3)]

    for way, piece in parts(1):
        if piece != 3:
            ring(way, 1, piece).start()
    for copy in near_copies:
        copy.start()
    for i in range(2):
        for copy in chunk_copies(i):
            copy.start()

    def box_coefficients(k):
        wide = jnp.concatenate([near_pair[4 * k + j].astype(BF) for j in range(4)], axis=1)
        box = dot_nn(wide, leaf_transfer[pl.ds(k * 8, 8)].reshape(512, 64))
        mine[LEAF + k] = side(box[:16], box[16:]).astype(BF)

    def pack_slots(off):
        fetch = pltpu.make_async_copy(tables.at[off], index.at[off], index_sem)
        fetch.start()
        fetch.wait()
        source = row(x, rem(z + off, NZ), c)

        def fill(k):
            d, q, dq = target(k)
            hi, lo = d // 8, rem(d, 8) * 16
            for j in range(SLOTS):
                tile = jnp.maximum(index[off, dq, hi, lo + j], 0)
                staged[k, off, j] = held[off][tile]
            return d, q

        @pl.loop(1, GROUP)
        def _(k):
            d, q = fill(k)
            remote(staged.at[k, off], recv.at[v, source], out_send, out_recv, d, q).start()

        fill(0)
        pltpu.make_async_copy(staged.at[0, off], recv.at[v, source], self_sem).start()

    def block_of(cc, xx):
        return (cc * NX + xx) * NZ

    def pack_boxes(off):
        place = block_of(c, x) + rem(z + off, NZ)
        source = held[off].at[pl.ds(LEAF, TOP)]
        for dx in range(1, NX):
            remote(
                source, every.at[place], every_send, every_recv.at[dx - 1],
                row(rem(x + dx, NX), z, c), v,
            ).start()
        remote(source, every.at[place], every_send, sibling_recv.at[0], sibling, v).start()
        pltpu.make_async_copy(source, every.at[place], every_self).start()
        for dx in range(NX):
            line = rem(x + dx, NX) * 2 + z // 4
            for q in range(NQ):
                rows_out[dx, rem(z + off, NZ), pl.ds(q, 1), :] = tables[off, q, pl.ds(line, 1), :]

    pack_slots(0)

    pl.loop(0, BOX)(box_coefficients)
    total = jnp.zeros((32, 64), F32)
    for k in range(0, BOX, 2):
        pair = join_tiles(mine[LEAF + k], mine[LEAF + k + 1])
        total += dot_nn(pair, box_transfer[pl.ds(k, 2)].reshape(128, 64))
    mine[LEAF + BOX] = side(total[:16], total[16:]).astype(BF)
    for way, piece in parts(1):
        if piece == 3:
            ring(way, 1, piece).start()
    pack_boxes(0)

    loads[4].wait()

    @pl.loop(0, BOX)
    def _(k):
        for m in range(2):
            shared[0, 2 * k + m] = side(box_raw[k, 2 * m], box_raw[k, 2 * m + 1])

    for step in range(1, NQ):
        remote(
            shared.at[0, pl.ds(0, 16)], shared.at[NQ - step, pl.ds(0, 16)],
            shared_send.at[0], shared_recv.at[0], me, rem(v + step, NQ),
        ).start()
    loads[3].wait()

    def chunk(i):
        for copy in chunk_copies(i):
            copy.wait()
        slot = i % 2

        @pl.loop(0, CHUNK // 2)
        def _(j):
            sides = []
            for t in range(2):
                l = 2 * j + t
                first = (i * CHUNK + l) * NEAR
                hi, lo = 3 + first // 128, rem(first, 128)
                left, right = [], []
                for n in range(0, NEAR, 2):
                    left.append(join_tiles(near[ints_s[hi, lo + n]], near[ints_s[hi, lo + n + 1]]))
                    right.append(side(near_raw[slot, l, n], near_raw[slot, l, n + 1]))
                sides.append(dot_nt(jnp.concatenate(left, axis=1), jnp.concatenate(right, axis=1)))
                for e in range(FL):
                    block = leaf_raw[slot, l, e]
                    weights[i * CHUNK + l, :, pl.ds(e * 128, 128)] = diag(block, block)
            near_pair[i * (CHUNK // 2) + j] = side(*sides)

        if i + 2 < LEAF // CHUNK:
            for copy in chunk_copies(i + 2):
                copy.start()

    for step in range(1, NZ // 2 + 1):
        for way, piece in parts(step):
            ring(way, step, piece).wait_recv()
            if step < NZ // 2 and (way, piece) in parts(step + 1):
                ring(way, step + 1, piece).start()
        offs = (NZ - step, step) if step < NZ // 2 else (step,)
        for off in offs:
            pack_boxes(off)
            pack_slots(off)
        if step == 1:
            for copy in near_copies:
                copy.wait_recv()
        if step < NZ // 2:
            chunk(step - 1)

    for k in range(1, NX * NC):
        dx, dc = k // NC, k % NC
        remote(
            rows_out.at[dx], rows_in.at[c * NX + x], rows_send, rows_recv,
            row(rem(x + dx, NX), z, rem(c + dc, NC)), v,
        ).start()
    rows_in[c * NX + x] = rows_out[0]
    chunk(3)

    loads[5].wait()
    levels = (me // 4, NROWS // 4 + me // 2, 3 * NROWS // 4 + me)
    line = lax.broadcasted_iota(I32, (8, 112), 0)
    node = lax.broadcasted_iota(I32, (8, 112), 1)
    chosen = jnp.zeros((8, 112), F32)
    for i, n in enumerate(levels):
        chosen = jnp.where((line == i) & (node == n), 1.0, chosen)
    chosen = chosen.astype(BF)

    @pl.loop(0, 64)
    def _(r):
        for e in range(2):
            picked[e, r] = dot_nt(chosen, coupling_raw[e, r])

    for i in range(3):
        shared[0, 16 + i] = side(picked[0, :, i, :], picked[1, :, i, :]).astype(BF)
    for step in range(1, NQ):
        remote(
            shared.at[0, pl.ds(16, 3)], shared.at[NQ - step, pl.ds(16, 3)],
            shared_send.at[1], shared_recv.at[1], me, rem(v + step, NQ),
        ).start()

    loads[6].wait()
    same = lax.broadcasted_iota(I32, (96, 96), 0) == lax.broadcasted_iota(I32, (96, 96), 1)
    eye = jnp.where(same, 1.0, 0.0).astype(BF)

    @pl.loop(0, 64)
    def _(r):
        coarse[r] = dot_nt(eye, coarse_raw[r])

    for dx in range(1, NX):
        here = every.at[pl.ds(block_of(c, rem(x + NX - dx, NX)), NZ)]
        settle(here, every_recv.at[dx - 1])
        remote(here, here, every_send, sibling_recv.at[dx], sibling, v).start()

    settle(staged.at[pl.ds(1, GROUP - 1)], out_recv)
    settle(staged.at[0], self_sem)

    @pl.loop(0, BOX)
    def _(k):
        for i in range(8):
            l = k * 8 + i
            left = []
            for e in range(FL):
                f = l * FL + e
                entry = ints_s[f // 128, rem(f, 128)]
                left.append(recv[:, entry // SLOTS, rem(entry, SLOTS)].reshape(64, 128))
            field = dot_nt(jnp.concatenate(left, axis=1), weights[l])
            part[:, l] = field.astype(BF).reshape(NQ, 16, 128)
        for step in range(1, NQ):
            q = rem(v + step, NQ)
            span = pl.ds(pl.multiple_of(k * 8, 8), 8)
            remote(
                part.at[q, span], arrived.at[step - 1, span], part_send, part_recv.at[k], me, q
            ).start()

    settle(lists.at[pl.ds(1, NQ - 1)], tab_recv.at[1])
    settle(shared.at[pl.ds(1, NQ - 1), pl.ds(0, 16)], shared_recv.at[0])
    settle(shared.at[pl.ds(1, NQ - 1), pl.ds(16, 3)], shared_recv.at[1])
    settle(rows_in.at[pl.ds(0, NX * NC - 1)], rows_recv)
    fetches = [
        pltpu.make_async_copy(lists, lists_s, load.at[0]),
        pltpu.make_async_copy(rows_in, rows_s, load.at[1]),
    ]
    for fetch in fetches:
        fetch.start()
    settle(every.at[pl.ds(0, NZ)], every_self)
    for dx in range(NX):
        settle(every.at[pl.ds(0, NZ)], sibling_recv.at[dx])
    for fetch in fetches:
        fetch.wait()

    def matrix(n):
        return coarse[:, n, :].astype(BF)

    def place_of(p):
        return block_of(rem(p, NC), p // (NC * NZ)) + rem(p // NC, NZ)

    @pl.loop(0, NROWS // 2)
    def _(n):
        pair = join_tiles(every[place_of(2 * n), BOX], every[place_of(2 * n + 1), BOX])
        pile = jnp.concatenate([matrix(32 + 2 * n), matrix(33 + 2 * n)], axis=0)
        upper[16 + n] = dot_nn(pair, pile).astype(BF)

    @pl.loop(0, NROWS // 4)
    def _(n):
        pair = side(upper[16 + 2 * n], upper[17 + 2 * n])
        pile = jnp.concatenate([matrix(2 * n), matrix(2 * n + 1)], axis=0)
        upper[n] = dot_nn(pair, pile).astype(BF)

    field = jnp.zeros((32, 64), F32)
    for level in range(3):
        if level == 1:
            field = dot_nt(field.astype(BF), matrix(me // 2))
        if level == 2:
            field = dot_nt(field.astype(BF), matrix(32 + me))
        for q in range(NQ):
            f = 32 + levels[level] * 2
            a, b = (lists_s[q, (f + e) // 128, rem(f + e, 128)] for e in range(2))
            if level < 2:
                pair = side(upper[a], upper[b])
            else:
                pair = join_tiles(every[place_of(jnp.maximum(a - 48, 0)), BOX], every[place_of(jnp.maximum(b - 48, 0)), BOX])
            field += dot_nt(pair, shared[q, 16 + level])
    root = field.astype(BF)
    column = (rem(z, 4) * 2 + c) * 16 + SLOTS

    @pl.loop(0, BOX)
    def _(k):
        left, right = [], []
        for q in range(NQ):
            for m in range(FB // 2):
                tiles = []
                for e in range(2):
                    entry = lists_s[q, 0, k * FB + 2 * m + e]
                    p = entry // 2
                    source = rem(p, NC) * NX + p // (NC * NZ)
                    zz = rem(p // NC, NZ)
                    number = rows_s[source, zz, q, column + rem(entry, 2)]
                    tiles.append(every[source * NZ + zz, jnp.maximum(number, 0)])
                left.append(join_tiles(*tiles))
                right.append(shared[q, 2 * k + m])
        box = dot_nt(root, box_transfer[k])
        box += dot_nt(jnp.concatenate(left, axis=1), jnp.concatenate(right, axis=1))
        wide = dot_nt(box.astype(BF), leaf_transfer[pl.ds(k * 8, 8)].reshape(512, 64))
        for j in range(4):
            base_pair[4 * k + j] = wide[:, j * 128 : (j + 1) * 128]

    @pl.loop(0, BOX)
    def _(k):
        span = pl.ds(pl.multiple_of(k * 8, 8), 8)
        settle(arrived.at[:, span], part_recv.at[k])
        for i in range(4):
            j = 4 * k + i
            fields = []
            for t in range(2):
                field = part[v, 2 * j + t].astype(F32)
                for step in range(NQ - 1):
                    field += arrived[step, 2 * j + t].astype(F32)
                fields.append(field)
            pair = (join_pair(*fields) + base_pair[j]).astype(BF)
            value = dot_nt(pair, basis_pair[j]) + near_pair[j]
            out[:, pl.ds(pl.multiple_of(j * 128, 128), 128)] = value.astype(BF)

    for step in range(1, NZ // 2 + 1):
        for way, piece in parts(step):
            ring(way, step, piece).wait_send()
    settle(tables.at[0, pl.ds(1, NQ - 1)], tab_send.at[0])
    settle(lists.at[pl.ds(1, NQ - 1)], tab_send.at[1])
    settle(staged.at[pl.ds(1, GROUP - 1)], out_send)
    settle(every.at[pl.ds(0, NZ * NX + NZ * (NX - 1))], every_send)
    settle(rows_in.at[pl.ds(0, NX * NC - 1)], rows_send)
    settle(shared.at[pl.ds(1, NQ - 1), pl.ds(0, 16)], shared_send.at[0])
    settle(shared.at[pl.ds(1, NQ - 1), pl.ds(16, 3)], shared_send.at[1])
    settle(arrived, part_send)
    for copy in near_copies:
        copy.wait_send()


def product(points, ints, *arrays):
    vmem, hbm = pl.BlockSpec(memory_space=pltpu.VMEM), pl.BlockSpec(memory_space=pl.ANY)
    dma = pltpu.SemaphoreType.DMA
    return pl.pallas_call(
        kernel,
        out_shape=jax.ShapeDtypeStruct((32, LEAF * 64), BF),
        in_specs=[vmem, vmem] + [hbm] * 8,
        out_specs=vmem,
        scratch_shapes=[
            *[pltpu.VMEM((TILES, 16, 128), BF)] * NZ,
            pltpu.VMEM((NZ, NQ, 8, 128), I32),
            pltpu.SMEM((NZ, NQ, 8, 128), I32),
            pltpu.VMEM((NQ, 8, 128), I32),
            pltpu.SMEM((NQ, 8, 128), I32),
            pltpu.SMEM((8, 128), I32),
            pltpu.VMEM((GROUP, NZ, SLOTS, 16, 128), BF),
            pltpu.VMEM((NQ, NROWS, SLOTS, 16, 128), BF),
            pltpu.VMEM((NROWS, TOP, 16, 128), BF),
            pltpu.VMEM((NX, NZ, NQ, 128), I32),
            pltpu.VMEM((NX * NC, NZ, NQ, 128), I32),
            pltpu.SMEM((NX * NC, NZ, NQ, 128), I32),
            pltpu.VMEM((3 * LEAF, 16, 128), BF),
            pltpu.VMEM((LEAF // 2, 32, 128), F32),
            pltpu.VMEM((LEAF // 2, 32, 128), F32),
            pltpu.VMEM((LEAF // 2, 128, 128), BF),
            pltpu.VMEM((LEAF, 128, FL * 128), BF),
            pltpu.VMEM((LEAF, 64, 64), BF),
            pltpu.VMEM((LEAF, 64, 64), BF),
            pltpu.VMEM((BOX, 64, 64), BF),
            pltpu.VMEM((BOX, FB, 64, 64), BF),
            pltpu.VMEM((64, 64, 96), BF),
            pltpu.VMEM((2, 64, 64, 112), BF),
            pltpu.VMEM((2, CHUNK, NEAR, 64, 64), BF),
            pltpu.VMEM((2, CHUNK, FL, 64, 64), BF),
            pltpu.VMEM((64, 96, 64), F32),
            pltpu.VMEM((2, 64, 8, 64), F32),
            pltpu.VMEM((NQ, 19, 64, 128), BF),
            pltpu.VMEM((48, 32, 64), BF),
            pltpu.VMEM((NQ, LEAF, 16, 128), BF),
            pltpu.VMEM((NQ - 1, LEAF, 16, 128), BF),
            dma((7,)),
            dma((2, 2)),
            dma((2,)),
            dma((2,)),
            dma((2, NZ // 2, 4)),
            dma((NZ, 4)),
            dma,
            dma,
            dma,
            dma((2,)),
            dma((2,)),
            dma,
            dma,
            dma((NX - 1,)),
            dma,
            dma((NX,)),
            dma,
            dma,
            dma((2,)),
            dma((2,)),
            dma,
            dma((BOX,)),
        ],
        compiler_params=pltpu.CompilerParams(
            collective_id=0, has_side_effects=True, vmem_limit_bytes=60 * 2**20
        ),
        name="product",
    )(points, ints, *arrays)


def body(
    points, basis, leaf_transfer, box_transfer, coarse_transfer, send_leaf, leaf_far, leaf_coupling,
    send_box, box_far, box_coupling, coarse_far, coarse_coupling, near_index, near_block,
):
    me = lax.axis_index("rows")
    local = jnp.clip(near_index - (me - 1) * LEAF, 0, 3 * LEAF - 1)
    table = jnp.concatenate([send_leaf, send_box, jnp.zeros((NROWS, 10), I32)], axis=1)
    ints = jnp.concatenate([
        table.reshape(-1), box_far.reshape(-1), coarse_far.reshape(-1), jnp.zeros((768,), I32),
        leaf_far.reshape(-1), local.reshape(-1), jnp.zeros((128,), I32),
    ]).reshape(24, 128)
    return product(
        points, ints, basis, leaf_transfer, box_transfer, leaf_coupling, box_coupling,
        coarse_transfer.transpose(1, 2, 0), coarse_coupling.transpose(1, 2, 3, 0), near_block,
    )


def solution(mesh):
    return jax.shard_map(
        body,
        mesh=mesh,
        in_specs=(
            P("cols", "rows"),
            P("rows", None, None),
            P("rows", None, None),
            P("rows", None, None),
            P(),
            P("rows", "cols"),
            P("rows", "cols"),
            P("rows", "cols", None, None),
            P("rows", "cols"),
            P("rows", "cols"),
            P("rows", "cols", None, None),
            P(None, "cols"),
            P(None, "cols", None, None),
            P("rows", None),
            P("rows", None, None, None),
        ),
        out_specs=P("cols", "rows"),
        check_vma=False,
    )
```

time: 372 us -> 116 us (0.31); the launches traced: 365 us -> 116 us
  local copies, waits for them, and re-layouts: 127 us -> 5.44 us
  waiting for transfers between devices: 118 us -> 0 us
  Pallas kernels: 0 us -> 109 us
  matrix products: 34.9 us -> 0 us
  starting transfers between devices: 30.6 us -> 0 us
  blocking collectives: 21.7 us -> 0 us
  other arithmetic: 18.2 us -> 1.46 us
  between operations: 15.6 us -> 0.04 us
    pallas_call x0 -> x1, Pallas kernels: none -> 109 us  [product(): pl.pallas_call(kernel, out_shape=jax.ShapeDtypeStruct((32, LEAF * 64), BF...]
    all_gather x2 -> x0, waiting for transfers between devices: 107 us -> none  [the longest x1 71.3 us: body(): roots_all = lax.all_gather(root_full[None], 'rows', axis=0, tiled=True)]
    gather x11 -> x0, local copies, waits for them, and re-layouts: 81.5 us -> none  [the longest x4 40.4 us: far_terms(): partner = jnp.take(received, slot_map.reshape(-1), axis=0)]
    dot_general x14 -> x0, matrix products: 34.9 us -> none  [the longest x2 10.8 us: far_terms(): jnp.einsum('lfrs,lfvs->lvr', coupling, partner, preferred_element_type=jn...]
    all_to_all x2 -> x0, starting transfers between devices: 25.7 us -> none  [the longest x1 14.7 us: body(): lax.all_to_all(outgoing(box_full, send_box), 'rows', split_axis=0, concat...]
    all_gather x2 -> x0, blocking collectives: 21.7 us -> none  [the longest x1 11.2 us: body(): lax.all_gather(boxes, 'cols', axis=1, tiled=True)]
    reshape x13 -> x5, local copies, waits for them, and re-layouts: 14.4 us -> 0.52 us  [the longest x1 0.14 us: body(): leaf_far.reshape(-1)]
    unnamed x38 -> x4, local copies, waits for them, and re-layouts: 14.8 us -> 3.99 us
  transfers between devices with their start and end apart: 7 -> 0, of which waited for: 5 -> 0; matrix products, arithmetic and copies ran while one was open for 28% -> 0% of each run, Pallas kernels for 0% -> 0%
where the time goes in v2:
time: 116 us
  Pallas kernels  109 us (94%)
  local copies, waits for them, and re-layouts  5.44 us (5%)
  other arithmetic  1.46 us (1%)
    pallas_call x1, Pallas kernels, product(): pl.pallas_call(kernel, out_shape=jax.ShapeDtypeStruct((32, LEAF * 64), BF...  109 us
    unnamed x4, local copies, waits for them, and re-layouts  3.99 us

profile of v2, /device:TPU:1, one launch (start us, length us, event | category | flops | bytes accessed | tf_op | source)
XLA Modules:
  0.0 115.9 jit_solution(9041357073439383959)
XLA Ops:
  0.0 0.1 pad.2.clone
  0.1 0.7 subtract_clamp_fusion
  0.8 0.8 copy.26
  1.5 0.1 reshape.19
  1.6 0.8 add_add_fusion
  2.4 0.1 copy.25
  2.5 0.1 reshape.18
  2.5 0.1 copy.29
  2.6 0.1 reshape.22
  2.7 0.8 copy.28
  3.5 0.1 reshape.21
  3.6 0.8 copy.27
  4.4 0.1 reshape.20
  4.6 0.7 concatenate.7
  5.3 108.9 %product.1 = bf16[32,4096]{1,0:T(8,128)(2,1)} custom-call(bf16[32,4096]{1,0:T(8,128)(2,1)} %points.1, s32[24,128]{1,0:T(8,128)} %bitcast.5, bf16[64,64,64]{2,1,0:T(8,128)(2,1)} %basis_h.1, bf16[64,64,64]{2,1,0:T(8,128)(2,1)} %leaf_h.1, bf16[8,64,64]{2,1,0:T(8,128)(2,1)} %box_h.1, bf16[64,6,64,64]{3,2,1,0:T(8,128)(2,1)} %leaf_coupling.1, ...), custom_call_target="tpu_custom_call" | custom-call | tf_op jit(solution)/shard_map/product/pallas_call | solution.py:486
  114.2 1.7 %copy.31 = bf16[32,4096]{1,0:T(8,128)(2,1)} copy(bf16[32,4096]{1,0:T(8,128)(2,1)} %product.1) | data formatting | bytes 524288
  (3 shorter events, 0.0 us)

commit v3 on v2

--- a/solution.py
+++ b/solution.py
@@ -13,7 +13,6 @@
 NROWS = NX * NZ * NC
 LEAF, BOX, NEAR = 64, 8, 8
 FL, FB = 6, 4
-TILES = LEAF + BOX + 1
 TOP = BOX + 1
 SLOTS = 4
 GROUP = NX * NC * NQ
@@ -61,21 +60,22 @@
 
 
 def kernel(
-    points, ints, basis_h, leaf_h, box_h, leaf_coupling, box_coupling, coarse_h, coarse_coupling,
+    points, send_leaf, send_box, box_far, coarse_far, leaf_far, near_index, basis_h, leaf_h, box_h, leaf_coupling, box_coupling, coarse_h, coarse_coupling,
     near_block, out, *scratch,
 ):
     held, scratch = scratch[:NZ], scratch[NZ:]
     (
-        tables, index, lists, lists_s, ints_s, staged, recv, every, rows_out, rows_in, rows_s,
+        raw, turned_raw, table, tables, compact, index, lists, lists_v, lists_s, leaf_s, near_s, staged, recv, every,
+        rows_in, rows_v, rows_s,
         near, near_pair, base_pair, basis_pair, weights,
         basis, leaf_transfer, box_transfer, box_raw, coarse_raw, coupling_raw, near_raw, leaf_raw,
         coarse, picked, shared, upper, part, arrived,
-    ) = scratch[:30]
+    ) = scratch[:36]
     (
         load, chunk_load, tab_send, tab_recv, ring_send, ring_recv, out_send, out_recv, self_sem,
-        near_send, near_recv, index_sem, every_send, every_recv, every_self, sibling_recv,
+        near_send, near_recv, index_sem, every_send, every_recv, sibling_recv, box_send, box_recv,
         rows_send, rows_recv, shared_send, shared_recv, part_send, part_recv,
-    ) = scratch[30:]
+    ) = scratch[36:]
     mine = held[0]
     me, v = lax.axis_index("rows"), lax.axis_index("cols")
     c = rem(me, NC)
@@ -102,8 +102,8 @@
         pltpu.make_async_copy(src, dst, load.at[i])
         for i, (src, dst) in enumerate((
             (basis_h, basis), (leaf_h, leaf_transfer), (box_h, box_transfer),
-            (ints.at[pl.ds(16, 8)], ints_s), (box_coupling, box_raw),
-            (coarse_coupling, coupling_raw), (coarse_h, coarse_raw),
+            (near_index, near_s), (box_coupling, box_raw),
+            (coarse_coupling, coupling_raw), (coarse_h, coarse_raw), (leaf_far, leaf_s),
         ))
     ]
     for copy in loads:
@@ -116,6 +116,10 @@
             pltpu.make_async_copy(leaf_coupling.at[part_of], leaf_raw.at[i % 2], chunk_load.at[1, i % 2]),
         )
 
+    for i in range(2):
+        for copy in chunk_copies(i):
+            copy.start()
+
     z_up, z_down = row(x, rem(z + 1, NZ), c), row(x, rem(z + NZ - 1, NZ), c)
     sibling = row(x, z, 1 - c)
     far_side = rem(me + 2 * c - 1 + NROWS, NROWS)
@@ -128,8 +132,22 @@
 
     for d in (z_up, z_down, far_side):
         pl.semaphore_signal(barrier, inc=1, device_id=(d, v), device_id_type=MESH)
-    tables[0, 0] = ints[pl.ds(0, 8)]
-    lists[0] = ints[pl.ds(8, 8)]
+    raw[...] = jnp.zeros((128, 128), I32)
+    raw[pl.ds(0, SLOTS), pl.ds(0, NROWS)] = send_leaf[...]
+    raw[pl.ds(SLOTS, 2), pl.ds(0, NROWS)] = send_box[...]
+    turned_raw[...] = jnp.transpose(raw[...])
+    lane = lax.broadcasted_iota(I32, (8, 128), 1)
+    rows = jnp.zeros((8, 128), I32)
+    for i in range(NX):
+        for j in range(NC):
+            column = i * 32 + j * 16
+            lines = turned_raw[pl.ds(i * NZ * NC + j, NZ, stride=NC), :]
+            rows = jnp.where((lane >= column) & (lane < column + 16), pltpu.roll(lines, column, 1), rows)
+    table[...] = rows
+    tables[0, 0] = rows
+    lists[0] = jnp.zeros((8, 128), I32)
+    lists[0, pl.ds(0, FB), pl.ds(0, BOX)] = box_far[...]
+    lists[0, pl.ds(FB, 2), pl.ds(0, 112)] = coarse_far[...]
 
     @pl.loop(0, LEAF // 2)
     def _(j):
@@ -138,21 +156,7 @@
         near[LEAF + 2 * j] = even.astype(BF)
         near[LEAF + 2 * j + 1] = odd.astype(BF)
 
-    pl.semaphore_wait(barrier, GROUP + 2)
-
-    for step in range(1, NQ):
-        q = rem(v + step, NQ)
-        remote(ints.at[pl.ds(0, 8)], tables.at[0, NQ - step], tab_send.at[0], tab_recv.at[0], me, q).start()
-        remote(ints.at[pl.ds(8, 8)], lists.at[NQ - step], tab_send.at[1], tab_recv.at[1], me, q).start()
-    own_near = near.at[pl.ds(LEAF, LEAF)]
-    near_copies = (
-        remote(own_near, near.at[pl.ds(0, LEAF)], near_send.at[0], near_recv.at[0], rem(me + 1, NROWS), v),
-        remote(own_near, near.at[pl.ds(2 * LEAF, LEAF)], near_send.at[1], near_recv.at[1], rem(me + NROWS - 1, NROWS), v),
-    )
-
     loads[0].wait()
-    loads[1].wait()
-    loads[2].wait()
 
     def coefficients(k):
         for j in range(4):
@@ -168,9 +172,19 @@
 
     pl.loop(0, BOX)(coefficients)
 
-    settle(tables.at[0, pl.ds(1, NQ - 1)], tab_recv.at[0])
-
-    PIECES = {0: pl.ds(0, 32), 1: pl.ds(32, 32), 3: pl.ds(LEAF, TOP)}
+    pl.semaphore_wait(barrier, GROUP + 2)
+
+    for step in range(1, NQ):
+        q = rem(v + step, NQ)
+        remote(table, tables.at[0, NQ - step], tab_send.at[0], tab_recv.at[0], me, q).start()
+        remote(lists.at[0], lists.at[NQ - step], tab_send.at[1], tab_recv.at[1], me, q).start()
+    own_near = near.at[pl.ds(LEAF, LEAF)]
+    near_copies = (
+        remote(own_near, near.at[pl.ds(0, LEAF)], near_send.at[0], near_recv.at[0], rem(me + 1, NROWS), v),
+        remote(own_near, near.at[pl.ds(2 * LEAF, LEAF)], near_send.at[1], near_recv.at[1], rem(me + NROWS - 1, NROWS), v),
+    )
+
+    PIECES = {0: pl.ds(0, 32), 1: pl.ds(32, 32)}
 
     def ring(way, step, piece):
         if way == 0:
@@ -187,34 +201,33 @@
 
     def parts(step):
         if step < NZ // 2:
-            return [(way, piece) for piece in (2, 0, 1, 3) for way in (0, 1)]
-        return [(0, 2), (0, 0), (1, 1), (1, 3)]
+            return [(way, piece) for piece in (2, 0, 1) for way in (0, 1)]
+        return [(0, 2), (0, 0), (1, 1)]
 
     for way, piece in parts(1):
-        if piece != 3:
+        if piece != 2:
             ring(way, 1, piece).start()
     for copy in near_copies:
         copy.start()
-    for i in range(2):
-        for copy in chunk_copies(i):
-            copy.start()
 
     def box_coefficients(k):
         wide = jnp.concatenate([near_pair[4 * k + j].astype(BF) for j in range(4)], axis=1)
         box = dot_nn(wide, leaf_transfer[pl.ds(k * 8, 8)].reshape(512, 64))
-        mine[LEAF + k] = side(box[:16], box[16:]).astype(BF)
+        every[place, k] = side(box[:16], box[16:]).astype(BF)
 
     def pack_slots(off):
-        fetch = pltpu.make_async_copy(tables.at[off], index.at[off], index_sem)
+        for q in range(NQ):
+            compact[rem(z + off, NZ), pl.ds(q, 1), :] = tables[off, q, pl.ds(z, 1), :]
+        fetch = pltpu.make_async_copy(compact.at[rem(z + off, NZ)], index.at[off], index_sem)
         fetch.start()
         fetch.wait()
         source = row(x, rem(z + off, NZ), c)
 
         def fill(k):
             d, q, dq = target(k)
-            hi, lo = d // 8, rem(d, 8) * 16
+            lo = rem(x + k // (NC * NQ), NX) * 32 + rem(c + rem(k // NQ, NC), NC) * 16
             for j in range(SLOTS):
-                tile = jnp.maximum(index[off, dq, hi, lo + j], 0)
+                tile = jnp.maximum(index[off, dq, lo + j], 0)
                 staged[k, off, j] = held[off][tile]
             return d, q
 
@@ -226,36 +239,34 @@
         fill(0)
         pltpu.make_async_copy(staged.at[0, off], recv.at[v, source], self_sem).start()
 
-    def block_of(cc, xx):
-        return (cc * NX + xx) * NZ
-
-    def pack_boxes(off):
-        place = block_of(c, x) + rem(z + off, NZ)
-        source = held[off].at[pl.ds(LEAF, TOP)]
-        for dx in range(1, NX):
-            remote(
-                source, every.at[place], every_send, every_recv.at[dx - 1],
-                row(rem(x + dx, NX), z, c), v,
-            ).start()
-        remote(source, every.at[place], every_send, sibling_recv.at[0], sibling, v).start()
-        pltpu.make_async_copy(source, every.at[place], every_self).start()
-        for dx in range(NX):
-            line = rem(x + dx, NX) * 2 + z // 4
-            for q in range(NQ):
-                rows_out[dx, rem(z + off, NZ), pl.ds(q, 1), :] = tables[off, q, pl.ds(line, 1), :]
-
-    pack_slots(0)
-
-    pl.loop(0, BOX)(box_coefficients)
-    total = jnp.zeros((32, 64), F32)
-    for k in range(0, BOX, 2):
-        pair = join_tiles(mine[LEAF + k], mine[LEAF + k + 1])
-        total += dot_nn(pair, box_transfer[pl.ds(k, 2)].reshape(128, 64))
-    mine[LEAF + BOX] = side(total[:16], total[16:]).astype(BF)
-    for way, piece in parts(1):
-        if piece == 3:
-            ring(way, 1, piece).start()
-    pack_boxes(0)
+    def block_of(cc, zz):
+        return (cc * NZ + zz) * NX
+
+    place = block_of(c, z) + x
+
+    def box_ring(way, step):
+        src = (NZ - step + 1) % NZ if way == 0 else step - 1
+        dst = NZ - step if way == 0 else step
+        block = every.at[pl.ds(block_of(c, rem(z + src, NZ)), NX)]
+        return remote(
+            block, block, box_send.at[way, step - 1], box_recv.at[dst], (z_up, z_down)[way], v
+        )
+
+    def box_ways(step):
+        return (0, 1) if step < NZ // 2 else (0,)
+
+    def box_step(step):
+        if step == 0:
+            settle(every.at[pl.ds(0, NX - 1)], every_recv)
+        else:
+            for way in box_ways(step):
+                box_ring(way, step).wait_recv()
+        if step < NZ // 2:
+            for way in box_ways(step + 1):
+                box_ring(way, step + 1).start()
+        for off in {0: (0,), NZ // 2: (NZ // 2,)}.get(step, (NZ - step, step)):
+            block = every.at[pl.ds(block_of(c, rem(z + off, NZ)), NX)]
+            remote(block, block, every_send, sibling_recv, sibling, v).start()
 
     loads[4].wait()
 
@@ -269,7 +280,27 @@
             shared.at[0, pl.ds(0, 16)], shared.at[NQ - step, pl.ds(0, 16)],
             shared_send.at[0], shared_recv.at[0], me, rem(v + step, NQ),
         ).start()
+    loads[1].wait()
+    loads[2].wait()
+    pl.loop(0, BOX)(box_coefficients)
+    total = jnp.zeros((32, 64), F32)
+    for k in range(0, BOX, 2):
+        pair = join_tiles(every[place, k], every[place, k + 1])
+        total += dot_nn(pair, box_transfer[pl.ds(k, 2)].reshape(128, 64))
+    every[place, BOX] = side(total[:16], total[16:]).astype(BF)
+    for dx in range(1, NX):
+        remote(
+            every.at[place], every.at[place], every_send, every_recv, row(rem(x + dx, NX), z, c), v
+        ).start()
+    settle(tables.at[0, pl.ds(1, NQ - 1)], tab_recv.at[0])
+    for way, piece in parts(1):
+        if piece == 2:
+            ring(way, 1, piece).start()
+    pack_slots(0)
     loads[3].wait()
+
+    def local(n, l):
+        return jnp.clip(near_s[n, l] - (me - 1) * LEAF, 0, 3 * LEAF - 1)
 
     def chunk(i):
         for copy in chunk_copies(i):
@@ -281,11 +312,10 @@
             sides = []
             for t in range(2):
                 l = 2 * j + t
-                first = (i * CHUNK + l) * NEAR
-                hi, lo = 3 + first // 128, rem(first, 128)
+                spot = i * CHUNK + l
                 left, right = [], []
                 for n in range(0, NEAR, 2):
-                    left.append(join_tiles(near[ints_s[hi, lo + n]], near[ints_s[hi, lo + n + 1]]))
+                    left.append(join_tiles(near[local(n, spot)], near[local(n + 1, spot)]))
                     right.append(side(near_raw[slot, l, n], near_raw[slot, l, n + 1]))
                 sides.append(dot_nt(jnp.concatenate(left, axis=1), jnp.concatenate(right, axis=1)))
                 for e in range(FL):
@@ -304,8 +334,8 @@
                 ring(way, step + 1, piece).start()
         offs = (NZ - step, step) if step < NZ // 2 else (step,)
         for off in offs:
-            pack_boxes(off)
             pack_slots(off)
+        box_step(step - 1)
         if step == 1:
             for copy in near_copies:
                 copy.wait_recv()
@@ -315,11 +345,12 @@
     for k in range(1, NX * NC):
         dx, dc = k // NC, k % NC
         remote(
-            rows_out.at[dx], rows_in.at[c * NX + x], rows_send, rows_recv,
+            compact, rows_in.at[c * NX + x], rows_send, rows_recv,
             row(rem(x + dx, NX), z, rem(c + dc, NC)), v,
         ).start()
-    rows_in[c * NX + x] = rows_out[0]
+    rows_in[c * NX + x] = compact[...]
     chunk(3)
+    box_step(NZ // 2)
 
     loads[5].wait()
     levels = (me // 4, NROWS // 4 + me // 2, 3 * NROWS // 4 + me)
@@ -351,11 +382,7 @@
     def _(r):
         coarse[r] = dot_nt(eye, coarse_raw[r])
 
-    for dx in range(1, NX):
-        here = every.at[pl.ds(block_of(c, rem(x + NX - dx, NX)), NZ)]
-        settle(here, every_recv.at[dx - 1])
-        remote(here, here, every_send, sibling_recv.at[dx], sibling, v).start()
-
+    loads[7].wait()
     settle(staged.at[pl.ds(1, GROUP - 1)], out_recv)
     settle(staged.at[0], self_sem)
 
@@ -365,8 +392,7 @@
             l = k * 8 + i
             left = []
             for e in range(FL):
-                f = l * FL + e
-                entry = ints_s[f // 128, rem(f, 128)]
+                entry = leaf_s[e, l]
                 left.append(recv[:, entry // SLOTS, rem(entry, SLOTS)].reshape(64, 128))
             field = dot_nt(jnp.concatenate(left, axis=1), weights[l])
             part[:, l] = field.astype(BF).reshape(NQ, 16, 128)
@@ -381,15 +407,20 @@
     settle(shared.at[pl.ds(1, NQ - 1), pl.ds(0, 16)], shared_recv.at[0])
     settle(shared.at[pl.ds(1, NQ - 1), pl.ds(16, 3)], shared_recv.at[1])
     settle(rows_in.at[pl.ds(0, NX * NC - 1)], rows_recv)
+    for q in range(NQ):
+        lists_v[pl.ds(8 * q, 8), :] = lists[q]
+    column = (x * NC + c) * 16 + SLOTS
+    for i in range(2):
+        block = rows_in[pl.ds(4 * i, 4)].reshape(128, 128)
+        turned = pltpu.roll(block, rem(128 - column, 128), 1)
+        rows_v[:, i * 128 : (i + 1) * 128] = jnp.transpose(turned)[:8]
     fetches = [
-        pltpu.make_async_copy(lists, lists_s, load.at[0]),
-        pltpu.make_async_copy(rows_in, rows_s, load.at[1]),
+        pltpu.make_async_copy(lists_v, lists_s, load.at[0]),
+        pltpu.make_async_copy(rows_v, rows_s, load.at[1]),
     ]
     for fetch in fetches:
         fetch.start()
-    settle(every.at[pl.ds(0, NZ)], every_self)
-    for dx in range(NX):
-        settle(every.at[pl.ds(0, NZ)], sibling_recv.at[dx])
+    settle(every.at[pl.ds(0, NX * NZ)], sibling_recv)
     for fetch in fetches:
         fetch.wait()
 
@@ -397,7 +428,7 @@
         return coarse[:, n, :].astype(BF)
 
     def place_of(p):
-        return block_of(rem(p, NC), p // (NC * NZ)) + rem(p // NC, NZ)
+        return block_of(rem(p, NC), rem(p // NC, NZ)) + p // (NC * NZ)
 
     @pl.loop(0, NROWS // 2)
     def _(n):
@@ -418,15 +449,13 @@
         if level == 2:
             field = dot_nt(field.astype(BF), matrix(32 + me))
         for q in range(NQ):
-            f = 32 + levels[level] * 2
-            a, b = (lists_s[q, (f + e) // 128, rem(f + e, 128)] for e in range(2))
+            a, b = (lists_s[8 * q + FB + e, levels[level]] for e in range(2))
             if level < 2:
                 pair = side(upper[a], upper[b])
             else:
                 pair = join_tiles(every[place_of(jnp.maximum(a - 48, 0)), BOX], every[place_of(jnp.maximum(b - 48, 0)), BOX])
             field += dot_nt(pair, shared[q, 16 + level])
     root = field.astype(BF)
-    column = (rem(z, 4) * 2 + c) * 16 + SLOTS
 
     @pl.loop(0, BOX)
     def _(k):
@@ -435,12 +464,12 @@
             for m in range(FB // 2):
                 tiles = []
                 for e in range(2):
-                    entry = lists_s[q, 0, k * FB + 2 * m + e]
+                    entry = lists_s[8 * q + 2 * m + e, k]
                     p = entry // 2
                     source = rem(p, NC) * NX + p // (NC * NZ)
                     zz = rem(p // NC, NZ)
-                    number = rows_s[source, zz, q, column + rem(entry, 2)]
-                    tiles.append(every[source * NZ + zz, jnp.maximum(number, 0)])
+                    number = rows_s[rem(entry, 2), (source * NZ + zz) * NQ + q]
+                    tiles.append(every[place_of(p), jnp.maximum(number, 0)])
                 left.append(join_tiles(*tiles))
                 right.append(shared[q, 2 * k + m])
         box = dot_nt(root, box_transfer[k])
@@ -471,7 +500,10 @@
     settle(tables.at[0, pl.ds(1, NQ - 1)], tab_send.at[0])
     settle(lists.at[pl.ds(1, NQ - 1)], tab_send.at[1])
     settle(staged.at[pl.ds(1, GROUP - 1)], out_send)
-    settle(every.at[pl.ds(0, NZ * NX + NZ * (NX - 1))], every_send)
+    settle(every.at[pl.ds(0, NZ * NX + NX - 1)], every_send)
+    for step in range(1, NZ // 2 + 1):
+        for way in box_ways(step):
+            box_ring(way, step).wait_send()
     settle(rows_in.at[pl.ds(0, NX * NC - 1)], rows_send)
     settle(shared.at[pl.ds(1, NQ - 1), pl.ds(0, 16)], shared_send.at[0])
     settle(shared.at[pl.ds(1, NQ - 1), pl.ds(16, 3)], shared_send.at[1])
@@ -480,27 +512,33 @@
         copy.wait_send()
 
 
-def product(points, ints, *arrays):
+def product(points, *arrays):
     vmem, hbm = pl.BlockSpec(memory_space=pltpu.VMEM), pl.BlockSpec(memory_space=pl.ANY)
     dma = pltpu.SemaphoreType.DMA
     return pl.pallas_call(
         kernel,
         out_shape=jax.ShapeDtypeStruct((32, LEAF * 64), BF),
-        in_specs=[vmem, vmem] + [hbm] * 8,
+        in_specs=[vmem] * 5 + [hbm] * 10,
         out_specs=vmem,
         scratch_shapes=[
-            *[pltpu.VMEM((TILES, 16, 128), BF)] * NZ,
+            *[pltpu.VMEM((LEAF, 16, 128), BF)] * NZ,
+            pltpu.VMEM((128, 128), I32),
+            pltpu.VMEM((128, 128), I32),
+            pltpu.VMEM((8, 128), I32),
             pltpu.VMEM((NZ, NQ, 8, 128), I32),
-            pltpu.SMEM((NZ, NQ, 8, 128), I32),
+            pltpu.VMEM((NZ, NQ, 128), I32),
+            pltpu.SMEM((NZ, NQ, 128), I32),
             pltpu.VMEM((NQ, 8, 128), I32),
-            pltpu.SMEM((NQ, 8, 128), I32),
-            pltpu.SMEM((8, 128), I32),
+            pltpu.VMEM((NQ * 8, 128), I32),
+            pltpu.SMEM((NQ * 8, 128), I32),
+            pltpu.SMEM((FL, LEAF), I32),
+            pltpu.SMEM((NEAR, LEAF), I32),
             pltpu.VMEM((GROUP, NZ, SLOTS, 16, 128), BF),
             pltpu.VMEM((NQ, NROWS, SLOTS, 16, 128), BF),
             pltpu.VMEM((NROWS, TOP, 16, 128), BF),
-            pltpu.VMEM((NX, NZ, NQ, 128), I32),
             pltpu.VMEM((NX * NC, NZ, NQ, 128), I32),
-            pltpu.SMEM((NX * NC, NZ, NQ, 128), I32),
+            pltpu.VMEM((8, 256), I32),
+            pltpu.SMEM((8, 256), I32),
             pltpu.VMEM((3 * LEAF, 16, 128), BF),
             pltpu.VMEM((LEAF // 2, 32, 128), F32),
             pltpu.VMEM((LEAF // 2, 32, 128), F32),
@@ -520,12 +558,12 @@
             pltpu.VMEM((48, 32, 64), BF),
             pltpu.VMEM((NQ, LEAF, 16, 128), BF),
             pltpu.VMEM((NQ - 1, LEAF, 16, 128), BF),
-            dma((7,)),
+            dma((8,)),
             dma((2, 2)),
             dma((2,)),
             dma((2,)),
-            dma((2, NZ // 2, 4)),
-            dma((NZ, 4)),
+            dma((2, NZ // 2, 3)),
+            dma((NZ, 3)),
             dma,
             dma,
             dma,
@@ -533,9 +571,10 @@
             dma((2,)),
             dma,
             dma,
-            dma((NX - 1,)),
-            dma,
-            dma((NX,)),
+            dma,
+            dma,
+            dma((2, NZ // 2)),
+            dma((NZ,)),
             dma,
             dma,
             dma((2,)),
@@ -547,23 +586,17 @@
             collective_id=0, has_side_effects=True, vmem_limit_bytes=60 * 2**20
         ),
         name="product",
-    )(points, ints, *arrays)
+    )(points, *arrays)
 
 
 def body(
     points, basis, leaf_transfer, box_transfer, coarse_transfer, send_leaf, leaf_far, leaf_coupling,
     send_box, box_far, box_coupling, coarse_far, coarse_coupling, near_index, near_block,
 ):
-    me = lax.axis_index("rows")
-    local = jnp.clip(near_index - (me - 1) * LEAF, 0, 3 * LEAF - 1)
-    table = jnp.concatenate([send_leaf, send_box, jnp.zeros((NROWS, 10), I32)], axis=1)
-    ints = jnp.concatenate([
-        table.reshape(-1), box_far.reshape(-1), coarse_far.reshape(-1), jnp.zeros((768,), I32),
-        leaf_far.reshape(-1), local.reshape(-1), jnp.zeros((128,), I32),
-    ]).reshape(24, 128)
     return product(
-        points, ints, basis, leaf_transfer, box_transfer, leaf_coupling, box_coupling,
-        coarse_transfer.transpose(1, 2, 0), coarse_coupling.transpose(1, 2, 3, 0), near_block,
+        points, send_leaf.T, send_box.T, box_far.T, coarse_far.T, leaf_far.T, near_index.T, basis, leaf_transfer, box_transfer,
+        leaf_coupling, box_coupling, coarse_transfer.transpose(1, 2, 0),
+        coarse_coupling.transpose(1, 2, 3, 0), near_block,
     )
 
 

time: 116 us -> 101 us (0.87)
  Pallas kernels: 109 us -> 98.9 us
  local copies, waits for them, and re-layouts: 5.44 us -> 1.67 us
  other arithmetic: 1.46 us -> 0 us
    pallas_call x1, Pallas kernels: 109 us -> 98.9 us  [product(): pl.pallas_call(kernel, out_shape=jax.ShapeDtypeStruct((32, LEAF * 64), BF...]
    unnamed x4 -> x1, local copies, waits for them, and re-layouts: 3.99 us -> 1.67 us
where the time goes in v3:
time: 101 us
  Pallas kernels  98.9 us (98%)
  local copies, waits for them, and re-layouts  1.67 us (2%)
    pallas_call x1, Pallas kernels, product(): pl.pallas_call(kernel, out_shape=jax.ShapeDtypeStruct((32, LEAF * 64), BF...  98.9 us

profile of v3, /device:TPU:1, one launch (start us, length us, event | category | flops | bytes accessed | tf_op | source)
XLA Modules:
  0.0 100.5 jit_solution(17778505778592869472)
XLA Ops:
  0.0 98.9 %product.1 = bf16[32,4096]{1,0:T(8,128)(2,1)} custom-call(bf16[32,4096]{1,0:T(8,128)(2,1)} %points.1, s32[4,64]{1,0:T(4,128)} %bitcast.12, s32[2,64]{1,0:T(2,128)} %bitcast.14, s32[4,8]{1,0:T(4,128)} %bitcast.13, s32[2,112]{1,0:T(2,128)} %bitcast.15, s32[6,64]{1,0:T(8,128)} %bitcast.10, s32[8,64]{1,0:T(8,128)} %bitcast.11, bf16[64,64,64]{2,1,0:T(8,128)(2,1)} %basis_h.1, ...), custom_call_target="tpu_custom_call" | custom-call | tf_op jit(solution)/shard_map/product/pallas_call | solution.py:518
  98.9 1.7 %copy.17 = bf16[32,4096]{1,0:T(8,128)(2,1)} copy(bf16[32,4096]{1,0:T(8,128)(2,1)} %product.1) | data formatting | bytes 524288

commit v4 on v3

--- a/solution.py
+++ b/solution.py
@@ -69,13 +69,13 @@
         rows_in, rows_v, rows_s,
         near, near_pair, base_pair, basis_pair, weights,
         basis, leaf_transfer, box_transfer, box_raw, coarse_raw, coupling_raw, near_raw, leaf_raw,
-        coarse, picked, shared, upper, part, arrived,
-    ) = scratch[:36]
+        coarse, piles, picked, shared, upper, part, arrived,
+    ) = scratch[:37]
     (
         load, chunk_load, tab_send, tab_recv, ring_send, ring_recv, out_send, out_recv, self_sem,
         near_send, near_recv, index_sem, every_send, every_recv, sibling_recv, box_send, box_recv,
         rows_send, rows_recv, shared_send, shared_recv, part_send, part_recv,
-    ) = scratch[36:]
+    ) = scratch[37:]
     mine = held[0]
     me, v = lax.axis_index("rows"), lax.axis_index("cols")
     c = rem(me, NC)
@@ -106,8 +106,7 @@
             (coarse_coupling, coupling_raw), (coarse_h, coarse_raw), (leaf_far, leaf_s),
         ))
     ]
-    for copy in loads:
-        copy.start()
+    loads[0].start()
 
     def chunk_copies(i):
         part_of = pl.ds(i * CHUNK, CHUNK)
@@ -115,10 +114,6 @@
             pltpu.make_async_copy(near_block.at[part_of], near_raw.at[i % 2], chunk_load.at[0, i % 2]),
             pltpu.make_async_copy(leaf_coupling.at[part_of], leaf_raw.at[i % 2], chunk_load.at[1, i % 2]),
         )
-
-    for i in range(2):
-        for copy in chunk_copies(i):
-            copy.start()
 
     z_up, z_down = row(x, rem(z + 1, NZ), c), row(x, rem(z + NZ - 1, NZ), c)
     sibling = row(x, z, 1 - c)
@@ -157,6 +152,11 @@
         near[LEAF + 2 * j + 1] = odd.astype(BF)
 
     loads[0].wait()
+    for copy in loads[1:]:
+        copy.start()
+    for i in range(2):
+        for copy in chunk_copies(i):
+            copy.start()
 
     def coefficients(k):
         for j in range(4):
@@ -215,9 +215,11 @@
         box = dot_nn(wide, leaf_transfer[pl.ds(k * 8, 8)].reshape(512, 64))
         every[place, k] = side(box[:16], box[16:]).astype(BF)
 
-    def pack_slots(off):
+    def read_rows(off):
         for q in range(NQ):
             compact[rem(z + off, NZ), pl.ds(q, 1), :] = tables[off, q, pl.ds(z, 1), :]
+
+    def pack_slots(off):
         fetch = pltpu.make_async_copy(compact.at[rem(z + off, NZ)], index.at[off], index_sem)
         fetch.start()
         fetch.wait()
@@ -275,11 +277,18 @@
         for m in range(2):
             shared[0, 2 * k + m] = side(box_raw[k, 2 * m], box_raw[k, 2 * m + 1])
 
-    for step in range(1, NQ):
-        remote(
-            shared.at[0, pl.ds(0, 16)], shared.at[NQ - step, pl.ds(0, 16)],
-            shared_send.at[0], shared_recv.at[0], me, rem(v + step, NQ),
-        ).start()
+    def share(way, hop):
+        step = 1 if way == 0 else NQ - 1
+        span = pl.ds(0, 16) if hop == 0 else pl.ds(8 * way, 8)
+        source, place_there = (0, NQ - step) if hop == 0 else (NQ - step, 2)
+        return remote(
+            shared.at[source, span], shared.at[place_there, span],
+            shared_send.at[1 + 2 * hop + way], shared_recv.at[1 + 2 * hop + way],
+            me, rem(v + step, NQ),
+        )
+
+    for way in range(2):
+        share(way, 0).start()
     loads[1].wait()
     loads[2].wait()
     pl.loop(0, BOX)(box_coefficients)
@@ -296,7 +305,31 @@
     for way, piece in parts(1):
         if piece == 2:
             ring(way, 1, piece).start()
+    read_rows(0)
     pack_slots(0)
+    box_step(0)
+    loads[5].wait()
+    levels = (me // 4, NROWS // 4 + me // 2, 3 * NROWS // 4 + me)
+    line = lax.broadcasted_iota(I32, (8, 112), 0)
+    node = lax.broadcasted_iota(I32, (8, 112), 1)
+    chosen = jnp.zeros((8, 112), F32)
+    for i, n in enumerate(levels):
+        chosen = jnp.where((line == i) & (node == n), 1.0, chosen)
+    chosen = chosen.astype(BF)
+
+    @pl.loop(0, 64)
+    def _(r):
+        for e in range(2):
+            picked[e, r] = dot_nt(chosen, coupling_raw[e, r])
+
+    for i in range(3):
+        shared[0, 16 + i] = side(picked[0, :, i, :], picked[1, :, i, :]).astype(BF)
+    for step in range(1, NQ):
+        remote(
+            shared.at[0, pl.ds(16, 3)], shared.at[NQ - step, pl.ds(16, 3)],
+            shared_send.at[0], shared_recv.at[0], me, rem(v + step, NQ),
+        ).start()
+
     loads[3].wait()
 
     def local(n, l):
@@ -334,45 +367,29 @@
                 ring(way, step + 1, piece).start()
         offs = (NZ - step, step) if step < NZ // 2 else (step,)
         for off in offs:
+            read_rows(off)
+        box_step(step)
+        if step == NZ // 2:
+            for k in range(1, NX * NC):
+                dx, dc = k // NC, k % NC
+                remote(
+                    compact, rows_in.at[c * NX + x], rows_send, rows_recv,
+                    row(rem(x + dx, NX), z, rem(c + dc, NC)), v,
+                ).start()
+            rows_in[c * NX + x] = compact[...]
+        for off in offs:
             pack_slots(off)
-        box_step(step - 1)
+        if step == 1:
+            for way in range(2):
+                share(way, 0).wait_recv()
+                share(way, 1).start()
         if step == 1:
             for copy in near_copies:
                 copy.wait_recv()
         if step < NZ // 2:
             chunk(step - 1)
 
-    for k in range(1, NX * NC):
-        dx, dc = k // NC, k % NC
-        remote(
-            compact, rows_in.at[c * NX + x], rows_send, rows_recv,
-            row(rem(x + dx, NX), z, rem(c + dc, NC)), v,
-        ).start()
-    rows_in[c * NX + x] = compact[...]
     chunk(3)
-    box_step(NZ // 2)
-
-    loads[5].wait()
-    levels = (me // 4, NROWS // 4 + me // 2, 3 * NROWS // 4 + me)
-    line = lax.broadcasted_iota(I32, (8, 112), 0)
-    node = lax.broadcasted_iota(I32, (8, 112), 1)
-    chosen = jnp.zeros((8, 112), F32)
-    for i, n in enumerate(levels):
-        chosen = jnp.where((line == i) & (node == n), 1.0, chosen)
-    chosen = chosen.astype(BF)
-
-    @pl.loop(0, 64)
-    def _(r):
-        for e in range(2):
-            picked[e, r] = dot_nt(chosen, coupling_raw[e, r])
-
-    for i in range(3):
-        shared[0, 16 + i] = side(picked[0, :, i, :], picked[1, :, i, :]).astype(BF)
-    for step in range(1, NQ):
-        remote(
-            shared.at[0, pl.ds(16, 3)], shared.at[NQ - step, pl.ds(16, 3)],
-            shared_send.at[1], shared_recv.at[1], me, rem(v + step, NQ),
-        ).start()
 
     loads[6].wait()
     same = lax.broadcasted_iota(I32, (96, 96), 0) == lax.broadcasted_iota(I32, (96, 96), 1)
@@ -381,6 +398,13 @@
     @pl.loop(0, 64)
     def _(r):
         coarse[r] = dot_nt(eye, coarse_raw[r])
+
+    def matrix(n):
+        return coarse[:, n, :].astype(BF)
+
+    @pl.loop(0, 48)
+    def _(n):
+        piles[n] = jnp.concatenate([matrix(2 * n), matrix(2 * n + 1)], axis=0)
 
     loads[7].wait()
     settle(staged.at[pl.ds(1, GROUP - 1)], out_recv)
@@ -404,8 +428,9 @@
             ).start()
 
     settle(lists.at[pl.ds(1, NQ - 1)], tab_recv.at[1])
-    settle(shared.at[pl.ds(1, NQ - 1), pl.ds(0, 16)], shared_recv.at[0])
-    settle(shared.at[pl.ds(1, NQ - 1), pl.ds(16, 3)], shared_recv.at[1])
+    for way in range(2):
+        share(way, 1).wait_recv()
+    settle(shared.at[pl.ds(1, NQ - 1), pl.ds(16, 3)], shared_recv.at[0])
     settle(rows_in.at[pl.ds(0, NX * NC - 1)], rows_recv)
     for q in range(NQ):
         lists_v[pl.ds(8 * q, 8), :] = lists[q]
@@ -424,23 +449,21 @@
     for fetch in fetches:
         fetch.wait()
 
-    def matrix(n):
-        return coarse[:, n, :].astype(BF)
-
     def place_of(p):
         return block_of(rem(p, NC), rem(p // NC, NZ)) + p // (NC * NZ)
 
-    @pl.loop(0, NROWS // 2)
-    def _(n):
-        pair = join_tiles(every[place_of(2 * n), BOX], every[place_of(2 * n + 1), BOX])
-        pile = jnp.concatenate([matrix(32 + 2 * n), matrix(33 + 2 * n)], axis=0)
-        upper[16 + n] = dot_nn(pair, pile).astype(BF)
-
-    @pl.loop(0, NROWS // 4)
-    def _(n):
-        pair = side(upper[16 + 2 * n], upper[17 + 2 * n])
-        pile = jnp.concatenate([matrix(2 * n), matrix(2 * n + 1)], axis=0)
-        upper[n] = dot_nn(pair, pile).astype(BF)
+    @pl.loop(0, NROWS // 16)
+    def _(m):
+        for i in range(8):
+            n = 8 * m + i
+            pair = join_tiles(every[place_of(2 * n), BOX], every[place_of(2 * n + 1), BOX])
+            upper[16 + n] = dot_nn(pair, piles[16 + n]).astype(BF)
+
+    @pl.loop(0, NROWS // 32)
+    def _(m):
+        for i in range(8):
+            n = 8 * m + i
+            upper[n] = dot_nn(side(upper[16 + 2 * n], upper[17 + 2 * n]), piles[n]).astype(BF)
 
     field = jnp.zeros((32, 64), F32)
     for level in range(3):
@@ -457,8 +480,7 @@
             field += dot_nt(pair, shared[q, 16 + level])
     root = field.astype(BF)
 
-    @pl.loop(0, BOX)
-    def _(k):
+    def box_field(k):
         left, right = [], []
         for q in range(NQ):
             for m in range(FB // 2):
@@ -478,6 +500,11 @@
         for j in range(4):
             base_pair[4 * k + j] = wide[:, j * 128 : (j + 1) * 128]
 
+    @pl.loop(0, 2)
+    def _(m):
+        for i in range(4):
+            box_field(4 * m + i)
+
     @pl.loop(0, BOX)
     def _(k):
         span = pl.ds(pl.multiple_of(k * 8, 8), 8)
@@ -505,8 +532,10 @@
         for way in box_ways(step):
             box_ring(way, step).wait_send()
     settle(rows_in.at[pl.ds(0, NX * NC - 1)], rows_send)
-    settle(shared.at[pl.ds(1, NQ - 1), pl.ds(0, 16)], shared_send.at[0])
-    settle(shared.at[pl.ds(1, NQ - 1), pl.ds(16, 3)], shared_send.at[1])
+    for way in range(2):
+        for hop in range(2):
+            share(way, hop).wait_send()
+    settle(shared.at[pl.ds(1, NQ - 1), pl.ds(16, 3)], shared_send.at[0])
     settle(arrived, part_send)
     for copy in near_copies:
         copy.wait_send()
@@ -553,6 +582,7 @@
             pltpu.VMEM((2, CHUNK, NEAR, 64, 64), BF),
             pltpu.VMEM((2, CHUNK, FL, 64, 64), BF),
             pltpu.VMEM((64, 96, 64), F32),
+            pltpu.VMEM((48, 128, 64), BF),
             pltpu.VMEM((2, 64, 8, 64), F32),
             pltpu.VMEM((NQ, 19, 64, 128), BF),
             pltpu.VMEM((48, 32, 64), BF),
@@ -577,8 +607,8 @@
             dma((NZ,)),
             dma,
             dma,
-            dma((2,)),
-            dma((2,)),
+            dma((5,)),
+            dma((5,)),
             dma,
             dma((BOX,)),
         ],

time: 101 us -> 93.7 us (0.928)
  Pallas kernels: 98.9 us -> 91.9 us
    pallas_call x1, Pallas kernels: 98.9 us -> 91.9 us  [product(): pl.pallas_call(kernel, out_shape=jax.ShapeDtypeStruct((32, LEAF * 64), BF...]
where the time goes in v4:
time: 93.7 us; the launch traced here: 93.6 us
  Pallas kernels  91.9 us (98%)
  local copies, waits for them, and re-layouts  1.67 us (2%)
    pallas_call x1, Pallas kernels, product(): pl.pallas_call(kernel, out_shape=jax.ShapeDtypeStruct((32, LEAF * 64), BF...  91.9 us

profile of v4, /device:TPU:1, one launch (start us, length us, event | category | flops | bytes accessed | tf_op | source)
XLA Modules:
  0.0 93.6 jit_solution(7744457461852584563)
XLA Ops:
  0.0 91.9 %product.1 = bf16[32,4096]{1,0:T(8,128)(2,1)} custom-call(bf16[32,4096]{1,0:T(8,128)(2,1)} %points.1, s32[4,64]{1,0:T(4,128)} %bitcast.12, s32[2,64]{1,0:T(2,128)} %bitcast.14, s32[4,8]{1,0:T(4,128)} %bitcast.13, s32[2,112]{1,0:T(2,128)} %bitcast.15, s32[6,64]{1,0:T(8,128)} %bitcast.10, s32[8,64]{1,0:T(8,128)} %bitcast.11, bf16[64,64,64]{2,1,0:T(8,128)(2,1)} %basis_h.1, ...), custom_call_target="tpu_custom_call" | custom-call | tf_op jit(solution)/shard_map/product/pallas_call | solution.py:547
  91.9 1.7 %copy.17 = bf16[32,4096]{1,0:T(8,128)(2,1)} copy(bf16[32,4096]{1,0:T(8,128)(2,1)} %product.1) | data formatting | bytes 524288

commit v5 on v4

--- a/solution.py
+++ b/solution.py
@@ -86,7 +86,7 @@
         return (xx * NZ + zz) * NC + cc
 
     def target(k):
-        dx, dc, dq = k // (NC * NQ), rem(k // NQ, NC), rem(k, NQ)
+        dx, dc, dq = rem(k, NX), k // (NX * NQ), rem(k + k // NX, NQ)
         return row(rem(x + dx, NX), z, rem(c + dc, NC)), rem(v + dq, NQ), dq
 
     def remote(src, dst, send, arrive, d, q):
@@ -227,7 +227,7 @@
 
         def fill(k):
             d, q, dq = target(k)
-            lo = rem(x + k // (NC * NQ), NX) * 32 + rem(c + rem(k // NQ, NC), NC) * 16
+            lo = rem(x + rem(k, NX), NX) * 32 + rem(c + k // (NX * NQ), NC) * 16
             for j in range(SLOTS):
                 tile = jnp.maximum(index[off, dq, lo + j], 0)
                 staged[k, off, j] = held[off][tile]
@@ -270,25 +270,6 @@
             block = every.at[pl.ds(block_of(c, rem(z + off, NZ)), NX)]
             remote(block, block, every_send, sibling_recv, sibling, v).start()
 
-    loads[4].wait()
-
-    @pl.loop(0, BOX)
-    def _(k):
-        for m in range(2):
-            shared[0, 2 * k + m] = side(box_raw[k, 2 * m], box_raw[k, 2 * m + 1])
-
-    def share(way, hop):
-        step = 1 if way == 0 else NQ - 1
-        span = pl.ds(0, 16) if hop == 0 else pl.ds(8 * way, 8)
-        source, place_there = (0, NQ - step) if hop == 0 else (NQ - step, 2)
-        return remote(
-            shared.at[source, span], shared.at[place_there, span],
-            shared_send.at[1 + 2 * hop + way], shared_recv.at[1 + 2 * hop + way],
-            me, rem(v + step, NQ),
-        )
-
-    for way in range(2):
-        share(way, 0).start()
     loads[1].wait()
     loads[2].wait()
     pl.loop(0, BOX)(box_coefficients)
@@ -301,6 +282,25 @@
         remote(
             every.at[place], every.at[place], every_send, every_recv, row(rem(x + dx, NX), z, c), v
         ).start()
+    loads[4].wait()
+
+    @pl.loop(0, BOX)
+    def _(k):
+        for m in range(2):
+            shared[0, 2 * k + m] = side(box_raw[k, 2 * m], box_raw[k, 2 * m + 1])
+
+    def share(way, hop):
+        step = 1 if way == 0 else NQ - 1
+        span = pl.ds(0, 16) if hop == 0 else pl.ds(8 * way, 8)
+        source, place_there = (0, NQ - step) if hop == 0 else (NQ - step, 2)
+        return remote(
+            shared.at[source, span], shared.at[place_there, span],
+            shared_send.at[1 + 2 * hop + way], shared_recv.at[1 + 2 * hop + way],
+            me, rem(v + step, NQ),
+        )
+
+    for way in range(2):
+        share(way, 0).start()
     settle(tables.at[0, pl.ds(1, NQ - 1)], tab_recv.at[0])
     for way, piece in parts(1):
         if piece == 2:

time: 93.7 us -> 93 us (level)
  no operation moved by 1% of the time
where the time goes in v5:
time: 93 us; the launch traced here: 92.9 us
  Pallas kernels  91.2 us (98%)
  local copies, waits for them, and re-layouts  1.67 us (2%)
    pallas_call x1, Pallas kernels, product(): pl.pallas_call(kernel, out_shape=jax.ShapeDtypeStruct((32, LEAF * 64), BF...  91.2 us

profile of v5, /device:TPU:1, one launch (start us, length us, event | category | flops | bytes accessed | tf_op | source)
XLA Modules:
  0.0 92.9 jit_solution(17388655271859788478)
XLA Ops:
  0.0 91.2 %product.1 = bf16[32,4096]{1,0:T(8,128)(2,1)} custom-call(bf16[32,4096]{1,0:T(8,128)(2,1)} %points.1, s32[4,64]{1,0:T(4,128)} %bitcast.12, s32[2,64]{1,0:T(2,128)} %bitcast.14, s32[4,8]{1,0:T(4,128)} %bitcast.13, s32[2,112]{1,0:T(2,128)} %bitcast.15, s32[6,64]{1,0:T(8,128)} %bitcast.10, s32[8,64]{1,0:T(8,128)} %bitcast.11, bf16[64,64,64]{2,1,0:T(8,128)(2,1)} %basis_h.1, ...), custom_call_target="tpu_custom_call" | custom-call | tf_op jit(solution)/shard_map/product/pallas_call | solution.py:547
  91.3 1.7 %copy.17 = bf16[32,4096]{1,0:T(8,128)(2,1)} copy(bf16[32,4096]{1,0:T(8,128)(2,1)} %product.1) | data formatting | bytes 524288
